TPU v7x, 256 devices: a whole 4x4x8 slice. The times are simulated.
256 devices in a mesh: rep: 64 (over y, z, x_hi), fsdp: 4 (over x_lo, core).
Axes of the slice: x: 4 (x_hi: 2, x_lo: 2; x = x_hi * 2 + x_lo), y: 4, z: 8, core: 2. Of those that a mesh axis runs over, the one named last changes fastest.
Arguments:
- local_weights: bfloat16 [64, 2, 1024, 4096], P('rep', None, 'fsdp'), may hold values from -16 to 16
- outer_weights: bfloat16 [2, 1024, 4096], P(None, 'fsdp'), may hold values from -6 to 6
- momentum: float32 [2, 1024, 4096], P(None, 'fsdp', 'rep'), may hold values from -6 to 6
- swa_mean: float32 [2, 1024, 4096], P(None, 'fsdp', 'rep'), may hold values from -6 to 6
- token_counts: int32 [64], P('rep'), may hold values from 262144 to 4194304, as said below
- swa_step: int32 [1], replicated, may hold values from 1 to 7
Outputs:
- new_weights: bfloat16 [2, 1024, 4096], P(None, 'fsdp')
- new_momentum: float32 [2, 1024, 4096], P(None, 'fsdp', 'rep')
- new_swa: float32 [2, 1024, 4096], P(None, 'fsdp', 'rep')
Inputs may be any that keep to these rules, and one draw needn't show every extreme that they name: `token_counts`: exactly one replica holds the largest count, 4194304 tokens; every other replica holds fewer.
All inputs are finite; a program needn't handle non-finite values.
Results may differ from a plain program's by a relative error of at most 0.0004.
Values may be sent and summed in bfloat16 or wider, within the bound.
A program may use at most 128 MiB of HBM per device.

v0:
```python
import jax
import jax.numpy as jnp
from jax import lax
from jax.sharding import PartitionSpec as P


def reduce_terms(terms):
    return lax.psum_scatter(terms, "rep", scatter_dimension=2, tiled=True)


def token_total(token_counts):
    summed = lax.psum(token_counts, "rep")
    return summed[0].astype(jnp.float32)


def per_device(local_weights, outer_weights, momentum, swa_mean, token_counts, swa_step):
    outer = outer_weights.astype(jnp.float32)
    difference = outer - local_weights[0].astype(jnp.float32)
    own_count = token_counts[0].astype(jnp.float32)
    total = token_total(token_counts)
    pseudo_grad = reduce_terms(own_count / total * difference)
    columns = outer.shape[2] // lax.axis_size("rep")
    start = lax.axis_index("rep") * columns
    outer_piece = lax.dynamic_slice_in_dim(outer, start, columns, 2)
    new_momentum = 0.9 * momentum + pseudo_grad
    updated = outer_piece - 0.7 * (pseudo_grad + 0.9 * new_momentum)
    divisor = swa_step[0].astype(jnp.float32) + 1.0
    new_swa = swa_mean + (updated - swa_mean) / divisor
    new_weights = lax.all_gather(updated.astype(jnp.bfloat16), "rep", axis=2, tiled=True)
    return (new_weights, new_momentum, new_swa)


def solution(mesh):
    return jax.shard_map(
        per_device,
        mesh=mesh,
        in_specs=(
            P("rep", None, "fsdp", None),
            P(None, "fsdp", None),
            P(None, "fsdp", "rep"),
            P(None, "fsdp", "rep"),
            P("rep"),
            P(),
        ),
        out_specs=(P(None, "fsdp", None), P(None, "fsdp", "rep"), P(None, "fsdp", "rep")),
        check_vma=False,
    )
```

profile of v0, /device:TPU:2, one launch (start us, length us, event | category | flops | bytes accessed | tf_op | source)
XLA Modules:
  0.0 571.4 jit_solution(4568938847496569489)
XLA Ops:
  7.2 0.0 reduce-scatter.2.cloned.1.call-start
  7.9 28.6 %psum.7 = s32[1]{0:T(128)} all-reduce(s32[1]{0:T(128)} %param.10), channel_id=1, replica_groups=mesh['rep'=64,'fsdp'=4] {'rep'}, use_global_device_ids=true, to_apply=%region_0.0 | all-reduce | flops 1 | bytes 8 | tf_op jit(solution)/shard_map/psum | solution.py:12
  36.4 6.3 %copy.9 = bf16[2,256,4096]{1,2,0:T(8,128)(2,1)} copy(bf16[2,256,4096]{2,1,0:T(8,128)(2,1)} %param.7) | data formatting | bytes 8388608 | tf_op args[1]
  42.8 6.3 %copy.10 = bf16[1,2,256,4096]{2,3,1,0:T(8,128)(2,1)} copy(bf16[1,2,256,4096]{3,2,1,0:T(8,128)(2,1)} %param.6) | data formatting | bytes 8388608 | tf_op args[0]
  49.8 7.8 %fusion = f32[2,256,4096]{1,2,0:T(8,128)} fusion(bf16[1,2,256,4096]{2,3,1,0:T(8,128)(2,1)} %copy.10, f32[]{:T(128)} %bitcast, bf16[2,256,4096]{1,2,0:T(8,128)(2,1)} %copy.9), kind=kLoop, calls=%fused_computation.1 | loop fusion | flops 8388608 | bytes 16777220 | tf_op jit(solution)/shard_map/mul | solution.py:21
  57.5 0.0 reduce-scatter.2.cloned.1.call-update
  57.6 0.0 copy-start
  57.6 0.0 copy-start.1
  57.6 0.0 all-gather.2.cloned.1.call-start
  57.6 6.1 %convert_element_type.24 = f32[2,256,4096]{1,2,0:T(8,128)} convert(bf16[2,256,4096]{1,2,0:T(8,128)(2,1)} %copy.9) | non-fusion elementwise | flops 2097152 | bytes 12582912 | tf_op jit(solution)/shard_map/convert_element_type | solution.py:17
  64.4 368.3 %reduce-scatter.2.cloned.1.call-done = f32[2,256,64]{1,2,0:T(8,128)} async-done(((f32[2,256,4096]{1,2,0:T(8,128)}), f32[2,256,64]{1,2,0:T(8,128)}) %reduce-scatter.2.cloned.1.call-update) | async-done | bytes 131088 | tf_op jit(solution)/shard_map/reduce_scatter | solution.py:8
  432.7 0.0 copy-done
  432.7 0.0 copy-done.1
  432.7 1.7 divide_add_fusion
  434.4 0.0 all-gather.2.cloned.1.call-update
  434.5 123.8 %all-gather.2.cloned.1.call-done = bf16[2,256,4096]{1,2,0:T(8,128)(2,1)} async-done(((bf16[2,256,64]{1,2,0:T(8,128)(2,1)}), bf16[2,256,4096]{1,2,0:T(8,128)(2,1)}) %all-gather.2.cloned.1.call-update) | async-done | bytes 4194320 | tf_op jit(solution)/shard_map/all_gather | solution.py:29
  558.2 6.3 %copy.11 = bf16[2,256,4096]{2,1,0:T(8,128)(2,1)} copy(bf16[2,256,4096]{1,2,0:T(8,128)(2,1)} %all-gather.2.cloned.1.call-done) | data formatting | bytes 8388608
Async XLA Ops:
  7.2 425.5 %reduce-scatter.2.cloned.1.call-start = ((), (), s32[]{:S(2)}) async-start(), calls=%async_computation.1 | async-start | bytes 8519680 | tf_op jit(solution)/shard_map/reduce_scatter | solution.py:8
  57.6 375.1 %copy-start = (f32[2,256,64]{1,2,0:T(8,128)S(1)}, f32[2,256,64]{1,2,0:T(8,128)}, u32[]{:S(2)}) copy-start(f32[2,256,64]{1,2,0:T(8,128)} %param.9) | copy-start | bytes 393220
  57.6 375.1 %copy-start.1 = (f32[2,256,64]{1,2,0:T(8,128)S(1)}, f32[2,256,64]{1,2,0:T(8,128)}, u32[]{:S(2)}) copy-start(f32[2,256,64]{1,2,0:T(8,128)} %param.8) | copy-start | bytes 393220
  57.6 500.6 %all-gather.2.cloned.1.call-start = ((), (), s32[]{:S(2)}) async-start(), calls=%async_computation.2 | async-start | bytes 4259840 | tf_op jit(solution)/shard_map/all_gather | solution.py:29
Sparse Core Ops, SparseCore 0:
  57.7 374.9 reduce-scatter.1
  436.8 121.3 all-gather.1
where the time goes:
time: 573 us; the launch traced here: 571 us
  waiting for transfers between devices  492 us (86%)
  blocking collectives  28.6 us (5%)
  local copies, waits for them, and re-layouts  19 us (3%)
  between operations  16.1 us (3%)
  other arithmetic  15.6 us (3%)
    reduce_scatter x1, waiting for transfers between devices, reduce_terms(): return lax.psum_scatter(terms, 'rep', scatter_dimension=2, tiled=True)  368 us
    all_gather x1, waiting for transfers between devices, per_device(): lax.all_gather(updated.astype(jnp.bfloat16), 'rep', axis=2, tiled=True)  124 us
    psum x1, blocking collectives, token_total(): summed = lax.psum(token_counts, 'rep')  28.6 us
    unnamed x7, local copies, waits for them, and re-layouts  19 us
  transfers between devices with their start and end apart: 2, of which 2 were waited for; matrix products, arithmetic and copies ran while one was open for 1% of the time, Pallas kernels for 0%

commit v1 on v0

v1 whole, which is shorter than its diff:
```python
import functools

import jax
import jax.numpy as jnp
from jax import lax
from jax.experimental import pallas as pl
from jax.experimental.pallas import tpu as pltpu
from jax.sharding import PartitionSpec as P

MESH = pl.DeviceIdType.MESH
NY, NZ, NX = 4, 8, 2
LANES = 128
R = 16
AHEAD = 3


def kernel(
    na, nd, rows,
    local, outer, mom_t, swa_t, tokens, step_no,
    out, nmom_t, nswa_t,
    a_raw, a_own, a_out, a_p, a_l, a_s, a_q, a_qx, a_w, a_wx, a_stage,
    d_raw, d_own, d_out, d_p, d_l, d_s, d_q, d_qy, d_w, d_stage,
    cnt, cnt_z, cnt_x, total, mbuf, sbuf, mfull, sfull, ofull, mback, sback,
    a_ss, a_rs, d_ss, d_rs, c_ss, c_rs, m_ss, m_rs, l_sem, o_sem,
):
    f32, bf16 = jnp.float32, jnp.bfloat16
    rep, fsdp = lax.axis_index("rep"), lax.axis_index("fsdp")
    y, z, x = rep // (NZ * NX), (rep // NX) % NZ, rep % NX
    other = 1 - x
    d_first = na * R

    def at(yy, zz, xx):
        return ((lax.rem(yy + 2 * NY, NY) * NZ + lax.rem(zz + 2 * NZ, NZ)) * NX + xx, fsdp)

    def zi(k):
        return lax.rem(z + k + 2 * NZ, NZ)

    def yi(k):
        return lax.rem(y + k + 2 * NY, NY)

    def remote(src, dst, ss, rs, where):
        return pltpu.make_async_remote_copy(
            src_ref=src, dst_ref=dst, send_sem=ss, recv_sem=rs, device_id=where, device_id_type=MESH
        )

    partner = at(y, z, other)
    y_peers = [at(y + k, z, x) for k in range(1, NY)]
    z_peers = [at(y, z + k, x) for k in range(1, NZ)]

    def a_rows(c):
        return pl.ds(pl.multiple_of(c * R, R), R)

    def d_rows(c):
        return pl.ds(pl.multiple_of(d_first + c * R, R), R)

    def count_y(k):
        return remote(cnt.at[0], cnt.at[k], c_ss.at[k], c_rs.at[k], y_peers[k - 1])

    def count_own_x():
        return remote(cnt.at[0], cnt.at[NY], c_ss.at[0], c_rs.at[0], partner)

    def count_z(k):
        return remote(cnt_z.at[0], cnt_z.at[k], c_ss.at[NY + k], c_rs.at[NY + k], z_peers[k - 1])

    def count_x():
        return remote(cnt_x.at[0], cnt_x.at[1], c_ss.at[NY], c_rs.at[NY], partner)

    half = pl.ds(pl.multiple_of(x * 64, 64), 64)
    other_half = pl.ds(pl.multiple_of(other * 64, 64), 64)

    def mom_in():
        return remote(mom_t.at[other], mbuf.at[half], m_ss.at[0], m_rs.at[0], partner)

    def swa_in():
        return remote(swa_t.at[other], sbuf.at[half], m_ss.at[1], m_rs.at[1], partner)

    def mom_back():
        return remote(mbuf.at[other_half], mback, m_ss.at[2], m_rs.at[2], partner)

    def swa_back():
        return remote(sbuf.at[other_half], sback, m_ss.at[3], m_rs.at[3], partner)

    ycols = pl.ds(pl.multiple_of(y * (NZ * LANES), NZ * LANES), NZ * LANES)
    cols = pl.ds(pl.multiple_of((y * NZ + z) * LANES, LANES), LANES)
    arows = pl.ds(0, na * R)
    drows = pl.ds(d_first, nd * R)
    loads = [
        pltpu.make_async_copy(outer.at[x, :, cols], ofull, l_sem.at[0]),
    ]
    if na:
        loads += [
            pltpu.make_async_copy(local.at[0, :, arows, ycols], a_own, l_sem.at[1]),
            pltpu.make_async_copy(outer.at[:, arows, ycols], a_out, l_sem.at[2]),
        ]
    if nd:
        loads += [
            pltpu.make_async_copy(local.at[0, x, drows, :], d_own, l_sem.at[3]),
            pltpu.make_async_copy(outer.at[x, drows, :], d_out, l_sem.at[4]),
        ]
    for load in loads:
        load.start()
    cnt[0] = jnp.full((8, LANES), tokens[0], jnp.int32)

    barrier = pltpu.get_barrier_semaphore()
    peers = y_peers + z_peers + [partner]
    for peer in peers:
        pl.semaphore_signal(barrier, inc=1, device_id=peer, device_id_type=MESH)
    pl.semaphore_wait(barrier, len(peers))

    def a_first(c, k):
        theirs = pl.ds(pl.multiple_of(yi(k) * (NZ * LANES), NZ * LANES), NZ * LANES)
        return remote(
            local.at[0, :, a_rows(c), theirs], a_raw.at[c, k - 1], a_ss.at[c, k - 1], a_rs.at[c, k - 1], y_peers[k - 1]
        )

    def d_first_copy(c):
        return remote(local.at[0, other, d_rows(c), :], d_raw.at[c], d_ss.at[c, 0], d_rs.at[c, 0], partner)

    def sums_up(c, sign, p, long, short, ss, rs, base):
        def way_l(k):
            src = p.at[c, zi(4 * sign)] if k == 0 else long.at[c, k - 1]
            return remote(src, long.at[c, k], ss.at[c, base + k], rs.at[c, base + k], at(y, z + sign, x))

        def way_s(k):
            src = p.at[c, zi(-3 * sign)] if k == 0 else short.at[c, k - 1]
            return remote(src, short.at[c, k], ss.at[c, base + 4 + k], rs.at[c, base + 4 + k], at(y, z - sign, x))

        return way_l, way_s

    def spread(c, sign, blocks, ss, rs, base):
        def way_l(k):
            block = blocks(c, zi(-k * sign))
            return remote(block, block, ss.at[c, base + k], rs.at[c, base + k], at(y, z + sign, x))

        def way_s(k):
            block = blocks(c, zi(k * sign))
            return remote(block, block, ss.at[c, base + 4 + k], rs.at[c, base + 4 + k], at(y, z - sign, x))

        def into_l(k):
            block = blocks(c, zi(-(k + 1) * sign))
            return remote(block, block, ss.at[c, base + k], rs.at[c, base + k], at(y, z + sign, x))

        def into_s(k):
            block = blocks(c, zi((k + 1) * sign))
            return remote(block, block, ss.at[c, base + 4 + k], rs.at[c, base + 4 + k], at(y, z - sign, x))

        return way_l, way_s, into_l, into_s

    def update(rws, pg_sum):
        o = ofull[rws, :].astype(f32)
        pg = pg_sum / total[0:1, :]
        nm = 0.9 * mfull[rws, :] + pg
        upd = o - 0.7 * (pg + 0.9 * nm)
        s = sfull[rws, :]
        divisor = step_no[0].astype(f32) + 1.0
        mfull[rws, :] = nm
        sfull[rws, :] = s + (upd - s) / divisor
        return upd.astype(bf16)

    def ring_stage(kind, stage, c, sign, p, long, short, ss, rs, base):
        way_l, way_s = sums_up(c, sign, p, long, short, ss, rs, base)
        if stage == 0:
            way_l(0).start()
            way_s(0).start()
            return
        k = stage - 1
        way_l(k).wait()
        if k < 3:
            long[c, k] += p[c, zi((3 - k) * sign)]
            way_l(k + 1).start()
            way_s(k).wait()
            if k < 2:
                short[c, k] += p[c, zi(-(2 - k) * sign)]
                way_s(k + 1).start()

    def spread_stage(stage, c, sign, blocks, ss, rs, base):
        way_l, way_s, into_l, into_s = spread(c, sign, blocks, ss, rs, base)
        if stage > 0:
            k = stage - 1
            into_l(k).wait_recv()
            if k < 3:
                into_s(k).wait_recv()
        if stage < 4:
            way_l(stage).start()
            if stage < 3:
                way_s(stage).start()
        if stage > 0:
            k = stage - 1
            way_l(k).wait_send()
            if k < 3:
                way_s(k).wait_send()

    def a_blocks(c, zz):
        return a_w.at[c, zz]

    def a_mid(c):
        return remote(a_q.at[c, other], a_qx.at[c], a_ss.at[c, 10], a_rs.at[c, 10], partner)

    def a_wy(c, k):
        mine = a_w.at[c, z, y]
        return remote(mine, mine, a_ss.at[c, 10 + k], a_rs.at[c, 10 + k], y_peers[k - 1])

    def a_wy_into(c, k):
        theirs = a_w.at[c, z, yi(-k)]
        return remote(theirs, theirs, a_ss.at[c, 10 + k], a_rs.at[c, 10 + k], y_peers[k - 1])

    def a_last(c):
        return remote(a_w.at[c], a_wx.at[c], a_ss.at[c, 21], a_rs.at[c, 21], partner)

    def a_store(c, m):
        return pltpu.make_async_copy(a_stage.at[c, m], out.at[m, a_rows(c), :], o_sem.at[c, m])

    def a_stage_fn(stage, c):
        sign = 1 - 2 * (c % 2)
        ring = functools.partial(ring_stage, "a", c=c, sign=sign, p=a_p, long=a_l, short=a_s, ss=a_ss, rs=a_rs, base=3)
        out_ring = functools.partial(spread_stage, c=c, sign=sign, blocks=a_blocks, ss=a_ss, rs=a_rs, base=14)
        if stage == 0:
            for k in range(1, NY):
                a_first(c, k).wait()
            for zz in range(NZ):
                sl = pl.ds(zz * LANES, LANES)
                for m in range(2):
                    o = a_out[m, a_rows(c), sl].astype(f32)
                    acc = cnt_f(0) * (o - a_own[m, a_rows(c), sl].astype(f32))
                    for k in range(1, NY):
                        acc += cnt_f(k) * (o - a_raw[c, k - 1, m, :, sl].astype(f32))
                    a_p[c, zz, m] = acc
            ring(0)
        elif stage <= 3:
            ring(stage)
        elif stage == 4:
            ring(4)
            a_q[c] = a_p[c, z] + a_l[c, 3] + a_s[c, 2]
            a_mid(c).start()
        elif stage == 5:
            a_mid(c).wait()
            a_w[c, z, y] = update(a_rows(c), a_q[c, x] + a_qx[c])
            for k in range(1, NY):
                a_wy(c, k).start()
        elif stage == 6:
            for k in range(1, NY):
                a_wy_into(c, k).wait_recv()
            out_ring(0)
            for k in range(1, NY):
                a_wy(c, k).wait_send()
        elif stage <= 9:
            out_ring(stage - 6)
        elif stage == 10:
            out_ring(4)
            a_last(c).start()
            for yy in range(NY):
                for zz in range(NZ):
                    a_stage[c, x, :, pl.ds((yy * NZ + zz) * LANES, LANES)] = a_w[c, zz, yy]
            a_store(c, x).start()
        else:
            a_last(c).wait()
            for yy in range(NY):
                for zz in range(NZ):
                    a_stage[c, other, :, pl.ds((yy * NZ + zz) * LANES, LANES)] = a_wx[c, zz, yy]
            a_store(c, other).start()

    def d_blocks(c, zz):
        return d_w.at[c, y, zz]

    def d_mid(c, k):
        return remote(d_q.at[c, yi(k)], d_qy.at[c, k - 1], d_ss.at[c, 7 + k], d_rs.at[c, 7 + k], y_peers[k - 1])

    def d_wx(c):
        mine = d_w.at[c, y, z, x]
        return remote(mine, mine, d_ss.at[c, 11], d_rs.at[c, 11], partner)

    def d_wx_into(c):
        theirs = d_w.at[c, y, z, other]
        return remote(theirs, theirs, d_ss.at[c, 11], d_rs.at[c, 11], partner)

    def d_last(c, k):
        mine = d_w.at[c, y]
        return remote(mine, mine, d_ss.at[c, 18 + k], d_rs.at[c, 18 + k], y_peers[k - 1])

    def d_last_into(c, k):
        theirs = d_w.at[c, yi(-k)]
        return remote(theirs, theirs, d_ss.at[c, 18 + k], d_rs.at[c, 18 + k], y_peers[k - 1])

    def d_store(c):
        return pltpu.make_async_copy(d_stage.at[c], out.at[:, d_rows(c), :], o_sem.at[na + c, 0])

    def d_stage_fn(stage, c):
        sign = 2 * (c % 2) - 1
        ring = functools.partial(ring_stage, "d", c=c, sign=sign, p=d_p, long=d_l, short=d_s, ss=d_ss, rs=d_rs, base=1)
        out_ring = functools.partial(spread_stage, c=c, sign=sign, blocks=d_blocks, ss=d_ss, rs=d_rs, base=12)
        if stage == 0:
            d_first_copy(c).wait()
            own = pl.ds(pl.multiple_of(c * R, R), R)
            for yy in range(NY):
                for zz in range(NZ):
                    sl = pl.ds((yy * NZ + zz) * LANES, LANES)
                    o = d_out[own, sl].astype(f32)
                    mine = cnt_f(0) * (o - d_own[own, sl].astype(f32))
                    d_p[c, zz, yy] = mine + cnt_f(NY) * (o - d_raw[c, :, sl].astype(f32))
            ring(0)
        elif stage <= 3:
            ring(stage)
        elif stage == 4:
            ring(4)
            d_q[c] = d_p[c, z] + d_l[c, 3] + d_s[c, 2]
            for k in range(1, NY):
                d_mid(c, k).start()
        elif stage == 5:
            for k in range(1, NY):
                d_mid(c, k).wait()
            d_w[c, y, z, x] = update(d_rows(c), d_q[c, y] + d_qy[c, 0] + d_qy[c, 1] + d_qy[c, 2])
            d_wx(c).start()
        elif stage == 6:
            d_wx_into(c).wait_recv()
            out_ring(0)
            d_wx(c).wait_send()
        elif stage <= 9:
            out_ring(stage - 6)
        elif stage == 10:
            out_ring(4)
            for k in range(1, NY):
                d_last(c, k).start()
        else:
            for k in range(1, NY):
                d_last_into(c, k).wait_recv()
            for yy in range(NY):
                for zz in range(NZ):
                    for m in range(2):
                        d_stage[c, m, :, pl.ds((yy * NZ + zz) * LANES, LANES)] = d_w[c, yy, zz, m]
            d_store(c).start()
            for k in range(1, NY):
                d_last(c, k).wait_send()

    def cnt_f(k):
        return cnt[k, 0:1, :].astype(f32)

    for k in range(1, NY):
        count_y(k).start()
    count_own_x().start()

    def send_first(c):
        if na:

            @pl.when(c < na)
            def _():
                for k in (2, 1, 3):
                    a_first(c, k).start()

        if nd:

            @pl.when(c < nd)
            def _():
                d_first_copy(c).start()

    for c in range(AHEAD):
        send_first(c)
    mom_in().start()
    swa_in().start()
    mbuf[half, :] = mom_t[x]
    sbuf[half, :] = swa_t[x]

    for k in range(1, NY):
        count_y(k).wait()
    count_own_x().wait()
    cnt_z[0] = cnt[0] + cnt[1] + cnt[2] + cnt[3]
    for k in range(1, NZ):
        count_z(k).start()
    for load in loads:
        load.wait()

    def slot(t, carry):
        @pl.when(t == 2)
        def _():
            for k in range(1, NZ):
                count_z(k).wait()
            acc = cnt_z[0]
            for k in range(1, NZ):
                acc += cnt_z[k]
            cnt_x[0] = acc
            count_x().start()

        @pl.when(t == 4)
        def _():
            count_x().wait()
            total[...] = (cnt_x[0] + cnt_x[1]).astype(f32)
            mom_in().wait()
            swa_in().wait()
            mfull[...] = mbuf[...].T
            sfull[...] = sbuf[...].T

        for stage in range(11, -1, -1):
            c = t - stage
            if na:
                pl.when((c >= 0) & (c < na))(functools.partial(a_stage_fn, stage, c))
            if nd:
                pl.when((c >= 0) & (c < nd))(functools.partial(d_stage_fn, stage, c))

        send_first(t + AHEAD)

        @pl.when(t == max(na, nd) + 5)
        def _():
            mbuf[...] = mfull[...].T
            sbuf[...] = sfull[...].T
            mom_back().start()
            swa_back().start()
            nmom_t[x] = mbuf[half, :]
            nswa_t[x] = sbuf[half, :]

        return carry

    lax.fori_loop(0, max(na, nd) + 11, slot, 0)
    mom_back().wait()
    swa_back().wait()
    nmom_t[other] = mback[...]
    nswa_t[other] = sback[...]

    def wait_out(c, carry):
        if na:

            @pl.when(c < na)
            def _():
                a_store(c, x).wait()
                a_store(c, other).wait()

        if nd:

            @pl.when(c < nd)
            def _():
                d_store(c).wait()

        return carry

    lax.fori_loop(0, max(na, nd), wait_out, 0)


def per_device(local, outer, momentum, swa, tokens, step_no):
    mats, rows, width = outer.shape
    na = rows // R // 2
    nd = rows // R - na
    f32, bf16, i32 = jnp.float32, jnp.bfloat16, jnp.int32
    vmem = pltpu.VMEM
    wide = NZ * LANES
    a, d = max(na, 1), max(nd, 1)
    scratch = [
        vmem((a, NY - 1, mats, R, wide), bf16),
        vmem((mats, a * R, wide), bf16),
        vmem((mats, a * R, wide), bf16),
        vmem((a, NZ, mats, R, LANES), f32),
        vmem((a, 4, mats, R, LANES), f32),
        vmem((a, 3, mats, R, LANES), f32),
        vmem((a, mats, R, LANES), f32),
        vmem((a, R, LANES), f32),
        vmem((a, NZ, NY, R, LANES), bf16),
        vmem((a, NZ, NY, R, LANES), bf16),
        vmem((a, mats, R, width), bf16),
        vmem((d, R, width), bf16),
        vmem((d * R, width), bf16),
        vmem((d * R, width), bf16),
        vmem((d, NZ, NY, R, LANES), f32),
        vmem((d, 4, NY, R, LANES), f32),
        vmem((d, 3, NY, R, LANES), f32),
        vmem((d, NY, R, LANES), f32),
        vmem((d, NY - 1, R, LANES), f32),
        vmem((d, NY, NZ, NX, R, LANES), bf16),
        vmem((d, mats, R, width), bf16),
        vmem((NY + 1, 8, LANES), i32),
        vmem((NZ, 8, LANES), i32),
        vmem((2, 8, LANES), i32),
        vmem((8, LANES), f32),
        vmem((LANES, rows), f32),
        vmem((LANES, rows), f32),
        vmem((rows, LANES), f32),
        vmem((rows, LANES), f32),
        vmem((rows, LANES), bf16),
        vmem((LANES // 2, rows), f32),
        vmem((LANES // 2, rows), f32),
        pltpu.SemaphoreType.DMA((a, 22)),
        pltpu.SemaphoreType.DMA((a, 22)),
        pltpu.SemaphoreType.DMA((d, 22)),
        pltpu.SemaphoreType.DMA((d, 22)),
        pltpu.SemaphoreType.DMA((NY + NZ,)),
        pltpu.SemaphoreType.DMA((NY + NZ,)),
        pltpu.SemaphoreType.DMA((4,)),
        pltpu.SemaphoreType.DMA((4,)),
        pltpu.SemaphoreType.DMA((5,)),
        pltpu.SemaphoreType.DMA((na + nd, 2)),
    ]
    anywhere = pl.BlockSpec(memory_space=pl.ANY)
    in_vmem = pl.BlockSpec(memory_space=pltpu.VMEM)
    in_smem = pl.BlockSpec(memory_space=pltpu.SMEM)
    turned = jax.ShapeDtypeStruct((mats, LANES // 2, rows), f32)
    new_weights, new_mom, new_swa = pl.pallas_call(
        functools.partial(kernel, na, nd, rows),
        out_shape=(jax.ShapeDtypeStruct(outer.shape, bf16), turned, turned),
        in_specs=[anywhere, anywhere, in_vmem, in_vmem, in_smem, in_smem],
        out_specs=(anywhere, in_vmem, in_vmem),
        scratch_shapes=scratch,
        compiler_params=pltpu.CompilerParams(
            collective_id=0, has_side_effects=True, vmem_limit_bytes=56 * 2**20
        ),
    )(local, outer, jnp.swapaxes(momentum, 1, 2), jnp.swapaxes(swa, 1, 2), tokens, step_no)
    return new_weights, jnp.swapaxes(new_mom, 1, 2), jnp.swapaxes(new_swa, 1, 2)


def solution(mesh):
    return jax.shard_map(
        per_device,
        mesh=mesh,
        in_specs=(
            P("rep", None, "fsdp", None),
            P(None, "fsdp", None),
            P(None, "fsdp", "rep"),
            P(None, "fsdp", "rep"),
            P("rep"),
            P(),
        ),
        out_specs=(P(None, "fsdp", None), P(None, "fsdp", "rep"), P(None, "fsdp", "rep")),
        check_vma=False,
    )
```

time: 573 us -> 117 us (0.20)
  waiting for transfers between devices: 492 us -> 0 us
  Pallas kernels: 0 us -> 108 us
  blocking collectives: 28.6 us -> 0 us
  other arithmetic: 15.6 us -> 0 us
  between operations: 16.1 us -> 1.95 us
  local copies, waits for them, and re-layouts: 19 us -> 6.06 us
    reduce_scatter x1 -> x0, waiting for transfers between devices: 368 us -> none  [reduce_terms(): return lax.psum_scatter(terms, 'rep', scatter_dimension=2, tiled=True)]
    all_gather x1 -> x0, waiting for transfers between devices: 124 us -> none  [per_device(): lax.all_gather(updated.astype(jnp.bfloat16), 'rep', axis=2, tiled=True)]
    pallas_call x0 -> x1, Pallas kernels: none -> 108 us  [per_device(): pl.pallas_call(functools.partial(kernel, na, nd, rows), out_shape=(jax.Sh...]
    psum x1 -> x0, blocking collectives: 28.6 us -> none  [token_total(): summed = lax.psum(token_counts, 'rep')]
    unnamed x7, local copies, waits for them, and re-layouts: 19 us -> 6.06 us
    mul x1 -> x0, other arithmetic: 7.77 us -> none  [per_device(): pseudo_grad = reduce_terms(own_count / total * difference)]
    convert_element_type x1 -> x0, other arithmetic: 6.13 us -> none  [per_device(): outer = outer_weights.astype(jnp.float32)]
  transfers between devices with their start and end apart: 2 -> 0, of which waited for: 2 -> 0; matrix products, arithmetic and copies ran while one was open for 1% -> 0% of each run, Pallas kernels for 0% -> 0%
where the time goes in v1:
time: 117 us; the launch traced here: 116 us
  Pallas kernels  108 us (92%)
  local copies, waits for them, and re-layouts  6.06 us (5%)
  between operations  1.95 us (2%)
    pallas_call x1, Pallas kernels, per_device(): pl.pallas_call(functools.partial(kernel, na, nd, rows), out_shape=(jax.Sh...  108 us
    unnamed x7, local copies, waits for them, and re-layouts  6.06 us

profile of v1, /device:TPU:2, one launch (start us, length us, event | category | flops | bytes accessed | tf_op | source)
XLA Modules:
  0.0 116.5 jit_solution(1376891786866608064)
XLA Ops:
  1.9 108.5 %shard_map.85 = (bf16[2,256,4096]{2,1,0:T(8,128)(2,1)}, f32[2,64,256]{2,1,0:T(8,128)}, f32[2,64,256]{2,1,0:T(8,128)}) custom-call(bf16[1,2,256,4096]{3,2,1,0:T(8,128)(2,1)} %local.1, bf16[2,256,4096]{2,1,0:T(8,128)(2,1)} %outer.1, f32[2,64,256]{2,1,0:T(8,128)} %bitcast.4, f32[2,64,256]{2,1,0:T(8,128)} %bitcast.5, s32[1]{0:T(128)S(6)} %copy.12.tokens, ...), custom_call_target="tpu_custom_call" | custom-call | tf_op jit(solution)/shard_map/pallas_call | solution.py:492
  110.4 0.0 copy-start.1
  110.4 0.0 copy-start
  110.4 4.7 %copy.14 = bf16[2,256,4096]{2,1,0:T(8,128)(2,1)} copy(bf16[2,256,4096]{2,1,0:T(8,128)(2,1)} %get-tuple-element.12) | data formatting | bytes 8388608
  115.1 0.0 copy-done.1
  115.1 0.7 copy.15
  115.8 0.0 copy-done
  115.8 0.7 copy.16
Async XLA Ops:
  110.4 4.8 %copy-start.1 = (f32[2,64,256]{2,1,0:T(8,128)S(1)}, f32[2,64,256]{2,1,0:T(8,128)}, u32[]{:S(2)}) copy-start(f32[2,64,256]{2,1,0:T(8,128)} %get-tuple-element.7) | copy-start | bytes 393220
  110.4 5.4 %copy-start = (f32[2,64,256]{2,1,0:T(8,128)S(1)}, f32[2,64,256]{2,1,0:T(8,128)}, u32[]{:S(2)}) copy-start(f32[2,64,256]{2,1,0:T(8,128)} %get-tuple-element.8) | copy-start | bytes 393220

commit v2 on v0

v2 whole, which is shorter than its diff:
```python
import functools

import jax
import jax.numpy as jnp
from jax import lax
from jax.experimental import pallas as pl
from jax.experimental.pallas import tpu as pltpu
from jax.sharding import PartitionSpec as P

MESH = pl.DeviceIdType.MESH
NY, NZ, NX = 4, 8, 2
LANES = 128
R = 16
AHEAD = 3
A_AT = tuple(range(9))
D_AT = tuple(range(9))
ORDER = tuple((kind, stage) for stage in range(9) for kind in "AD")
RAW, RING, MID, FIRST, SECOND, LAST = 0, 1, 5, 6, 7, 8


def kernel(
    na, nd, rows,
    local, outer, mom_t, swa_t, tokens, step_no,
    out, nmom_t, nswa_t,
    a_raw, a_own, a_out, a_p, a_r, a_q, a_qx, a_w, a_wx, a_stage,
    d_raw, d_own, d_out, d_p, d_r, d_q, d_qy, d_w, d_stage,
    cnt, cnt_z, cnt_x, total, mbuf, sbuf, mfull, sfull, ofull,
    a_ss, a_rs, d_ss, d_rs, raw_ss, c_ss, c_rs, m_ss, m_rs, l_sem, o_sem,
):
    f32, bf16 = jnp.float32, jnp.bfloat16
    rep, fsdp = lax.axis_index("rep"), lax.axis_index("fsdp")
    y, z, x = rep // (NZ * NX), (rep // NX) % NZ, rep % NX
    other = 1 - x
    d_row = na * R

    def at(yy, zz, xx):
        return ((lax.rem(yy + 2 * NY, NY) * NZ + lax.rem(zz + 2 * NZ, NZ)) * NX + xx, fsdp)

    def zi(k):
        return lax.rem(z + k + 2 * NZ, NZ)

    def yi(k):
        return lax.rem(y + k + 2 * NY, NY)

    def send(src, dst, ss, rs, where):
        pltpu.make_async_remote_copy(
            src_ref=src, dst_ref=dst, send_sem=ss, recv_sem=rs, device_id=where, device_id_type=MESH
        ).start()

    def drain(ref, sem):
        pltpu.make_async_copy(ref, ref, sem).wait()

    partner = at(y, z, other)
    y_peers = [at(y + k, z, x) for k in range(1, NY)]
    z_peers = [at(y, z + k, x) for k in range(1, NZ)]

    def a_rows(c):
        return pl.ds(pl.multiple_of(c * R, R), R)

    def d_rows(c):
        return pl.ds(pl.multiple_of(d_row + c * R, R), R)

    def lanes(block):
        return pl.ds(block * LANES, LANES)

    def cnt_f(k):
        return cnt[k, 0:1, :].astype(f32)

    half = pl.ds(pl.multiple_of(x * (LANES // 2), LANES // 2), LANES // 2)
    other_half = pl.ds(pl.multiple_of(other * (LANES // 2), LANES // 2), LANES // 2)
    ycols = pl.ds(pl.multiple_of(y * (NZ * LANES), NZ * LANES), NZ * LANES)
    cols = pl.ds(pl.multiple_of((y * NZ + z) * LANES, LANES), LANES)
    arows, drows = pl.ds(0, na * R), pl.ds(d_row, nd * R)
    loads = [
        pltpu.make_async_copy(local.at[0, :, arows, ycols], a_own, l_sem.at[1]),
        pltpu.make_async_copy(outer.at[:, arows, ycols], a_out, l_sem.at[2]),
        pltpu.make_async_copy(local.at[0, x, drows, :], d_own, l_sem.at[3]),
        pltpu.make_async_copy(outer.at[x, drows, :], d_out, l_sem.at[4]),
    ]
    late_loads = [
        pltpu.make_async_copy(outer.at[x, :, cols], ofull, l_sem.at[0]),
        pltpu.make_async_copy(mom_t.at[x], mbuf.at[half], l_sem.at[5]),
        pltpu.make_async_copy(swa_t.at[x], sbuf.at[half], l_sem.at[6]),
    ]
    for load in loads + late_loads:
        load.start()
    cnt[0] = jnp.full((8, LANES), tokens[0], jnp.int32)

    barrier = pltpu.get_barrier_semaphore()
    peers = y_peers + z_peers + [partner]
    for peer in peers:
        pl.semaphore_signal(barrier, inc=1, device_id=peer, device_id_type=MESH)
    pl.semaphore_wait(barrier, len(peers))

    def send_raw(c):
        @pl.when(c < na)
        def _():
            for k in (2, 1, 3):
                theirs = pl.ds(pl.multiple_of(yi(k) * (NZ * LANES), NZ * LANES), NZ * LANES)
                send(
                    local.at[0, :, a_rows(c), theirs], a_raw.at[c, k - 1],
                    raw_ss.at[0, c % 4], a_rs.at[c, RAW], y_peers[k - 1],
                )

        @pl.when(c < nd)
        def _():
            send(local.at[0, other, d_rows(c), :], d_raw.at[c], raw_ss.at[1, c % 4], d_rs.at[c, RAW], partner)

    def ring_stage(stage, c, sign, p, r, ss, rs):
        up, down = at(y, z + sign, x), at(y, z - sign, x)

        def step(k, long, short):
            send(long, r.at[c, k, 0], ss.at[c % 2, RING + k], rs.at[c, RING + k], up)
            if k < 3:
                send(short, r.at[c, k, 1], ss.at[c % 2, RING + k], rs.at[c, RING + k], down)

        if stage == 0:
            step(0, p.at[c, zi(4 * sign)], p.at[c, zi(-3 * sign)])
            return
        k = stage - 1
        came = r.at[c, k] if k < 3 else r.at[c, k, 0]
        drain(came, rs.at[c, RING + k])
        if k < 3:
            r[c, k, 0] += p[c, zi((3 - k) * sign)]
            if k < 2:
                r[c, k, 1] += p[c, zi(-(2 - k) * sign)]
            step(k + 1, r.at[c, k, 0], r.at[c, k, 1])
        drain(came, ss.at[c % 2, RING + k])

    def update(rws, pg_sum):
        o = ofull[rws, :].astype(f32)
        pg = pg_sum / total[0:1, :]
        nm = 0.9 * mfull[rws, :] + pg
        upd = o - 0.7 * (pg + 0.9 * nm)
        s = sfull[rws, :]
        divisor = step_no[0].astype(f32) + 1.0
        mfull[rws, :] = nm
        sfull[rws, :] = s + (upd - s) / divisor
        return upd.astype(bf16)

    def a_store(c, m):
        return pltpu.make_async_copy(a_stage.at[c, m], out.at[m, a_rows(c), :], o_sem.at[c, m])

    def a_stage_fn(stage, c):
        ring = functools.partial(ring_stage, c=c, sign=1 - 2 * (c % 2), p=a_p, r=a_r, ss=a_ss, rs=a_rs)

        def sems(k):
            return a_ss.at[c % 2, k], a_rs.at[c, k]

        def landed(ref, k):
            drain(ref, a_rs.at[c, k])

        def left(ref, k):
            drain(ref, a_ss.at[c % 2, k])

        if stage == 0:
            landed(a_raw.at[c], RAW)
            for zz in range(NZ):
                for m in range(2):
                    o = a_out[m, a_rows(c), lanes(zz)].astype(f32)
                    acc = cnt_f(0) * (o - a_own[m, a_rows(c), lanes(zz)].astype(f32))
                    for k in range(1, NY):
                        acc += cnt_f(k) * (o - a_raw[c, k - 1, m, :, lanes(zz)].astype(f32))
                    a_p[c, zz, m] = acc
            ring(0)
            drain(a_raw.at[c], raw_ss.at[0, c % 4])
        elif stage <= 3:
            ring(stage)
        elif stage == 4:
            ring(4)
            a_q[c] = a_p[c, z] + a_r[c, 3, 0] + a_r[c, 2, 1]
            send(a_q.at[c, other], a_qx.at[c], *sems(MID), partner)
        elif stage == 5:
            landed(a_qx.at[c], MID)
            mine = a_w.at[c, y, z]
            mine[...] = update(a_rows(c), a_q[c, x] + a_qx[c])
            for k in (4, 3, 5, 2, 6, 1, 7):
                send(mine, mine, *sems(FIRST), z_peers[k - 1])
            left(a_qx.at[c], MID)
        elif stage == 6:
            landed(a_w.at[c, y, pl.ds(0, NZ - 1)], FIRST)
            mine = a_w.at[c, y]
            for k in (2, 1, 3):
                send(mine, mine, *sems(SECOND), y_peers[k - 1])
            left(a_w.at[c, y, pl.ds(0, NZ - 1)], FIRST)
        elif stage == 7:
            landed(a_w.at[c, pl.ds(0, NY - 1)], SECOND)
            send(a_w.at[c], a_wx.at[c], *sems(LAST), partner)
            for yy in range(NY):
                for zz in range(NZ):
                    a_stage[c, x, :, lanes(yy * NZ + zz)] = a_w[c, yy, zz]
            a_store(c, x).start()
            left(a_w.at[c, pl.ds(0, NY - 1)], SECOND)
        else:
            landed(a_wx.at[c], LAST)
            for yy in range(NY):
                for zz in range(NZ):
                    a_stage[c, other, :, lanes(yy * NZ + zz)] = a_wx[c, yy, zz]
            a_store(c, other).start()
            left(a_wx.at[c], LAST)

    def d_store(c):
        return pltpu.make_async_copy(d_stage.at[c], out.at[:, d_rows(c), :], o_sem.at[na + c, 0])

    def d_stage_fn(stage, c):
        ring = functools.partial(ring_stage, c=c, sign=2 * (c % 2) - 1, p=d_p, r=d_r, ss=d_ss, rs=d_rs)

        def sems(k):
            return d_ss.at[c % 2, k], d_rs.at[c, k]

        def landed(ref, k):
            drain(ref, d_rs.at[c, k])

        def left(ref, k):
            drain(ref, d_ss.at[c % 2, k])

        if stage == 0:
            landed(d_raw.at[c], RAW)
            own = pl.ds(pl.multiple_of(c * R, R), R)
            for yy in range(NY):
                for zz in range(NZ):
                    sl = lanes(yy * NZ + zz)
                    o = d_out[own, sl].astype(f32)
                    mine = cnt_f(0) * (o - d_own[own, sl].astype(f32))
                    d_p[c, zz, yy] = mine + cnt_f(NY) * (o - d_raw[c, :, sl].astype(f32))
            ring(0)
            drain(d_raw.at[c], raw_ss.at[1, c % 4])
        elif stage <= 3:
            ring(stage)
        elif stage == 4:
            ring(4)
            d_q[c] = d_p[c, z] + d_r[c, 3, 0] + d_r[c, 2, 1]
            for k in (2, 1, 3):
                send(d_q.at[c, yi(k)], d_qy.at[c, k - 1], *sems(MID), y_peers[k - 1])
        elif stage == 5:
            landed(d_qy.at[c], MID)
            mine = d_w.at[c, y, x, z]
            mine[...] = update(d_rows(c), d_q[c, y] + d_qy[c, 0] + d_qy[c, 1] + d_qy[c, 2])
            for k in (4, 3, 5, 2, 6, 1, 7):
                send(mine, mine, *sems(FIRST), z_peers[k - 1])
            left(d_qy.at[c], MID)
        elif stage == 6:
            landed(d_w.at[c, y, x, pl.ds(0, NZ - 1)], FIRST)
            mine = d_w.at[c, y, x]
            send(mine, mine, *sems(SECOND), partner)
            left(d_w.at[c, y, x, pl.ds(0, NZ - 1)], FIRST)
        elif stage == 7:
            landed(d_w.at[c, y, other], SECOND)
            mine = d_w.at[c, y]
            for k in (2, 1, 3):
                send(mine, mine, *sems(LAST), y_peers[k - 1])
            left(d_w.at[c, y, x], SECOND)
        else:
            landed(d_w.at[c, pl.ds(0, NY - 1)], LAST)
            for yy in range(NY):
                for zz in range(NZ):
                    for m in range(2):
                        d_stage[c, m, :, lanes(yy * NZ + zz)] = d_w[c, yy, m, zz]
            d_store(c).start()
            left(d_w.at[c, pl.ds(0, NY - 1)], LAST)

    for k in range(1, NY):
        send(cnt.at[0], cnt.at[k], c_ss.at[0], c_rs.at[0], y_peers[k - 1])
    send(cnt.at[0], cnt.at[NY], c_ss.at[0], c_rs.at[0], partner)
    for c in range(AHEAD):
        send_raw(c)
    send(mom_t.at[other], mbuf.at[half], m_ss.at[0], m_rs.at[0], partner)
    send(swa_t.at[other], sbuf.at[half], m_ss.at[0], m_rs.at[1], partner)
    drain(cnt.at[pl.ds(0, NY)], c_rs.at[0])
    drain(cnt.at[pl.ds(0, NY)], c_ss.at[0])
    cnt_z[0] = cnt[0] + cnt[1] + cnt[2] + cnt[3]
    for k in range(1, NZ):
        send(cnt_z.at[0], cnt_z.at[k], c_ss.at[1], c_rs.at[1], z_peers[k - 1])
    for load in loads:
        load.wait()

    def slot(t, carry):
        @pl.when(t == 2)
        def _():
            drain(cnt_z.at[pl.ds(0, NZ - 1)], c_rs.at[1])
            drain(cnt_z.at[pl.ds(0, NZ - 1)], c_ss.at[1])
            acc = cnt_z[0]
            for k in range(1, NZ):
                acc += cnt_z[k]
            cnt_x[0] = acc
            send(cnt_x.at[0], cnt_x.at[1], c_ss.at[2], c_rs.at[2], partner)

        @pl.when(t == 4)
        def _():
            drain(cnt_x.at[0], c_rs.at[2])
            drain(cnt_x.at[0], c_ss.at[2])
            total[...] = (cnt_x[0] + cnt_x[1]).astype(f32)
            drain(mbuf.at[other_half], m_rs.at[0])
            drain(sbuf.at[other_half], m_rs.at[1])
            drain(mbuf, m_ss.at[0])
            for load in late_loads:
                load.wait()
            mfull[...] = mbuf[...].T
            sfull[...] = sbuf[...].T

        for kind, stage in ORDER:
            first, count, fn = (A_AT, na, a_stage_fn) if kind == "A" else (D_AT, nd, d_stage_fn)
            c = t - first[stage]
            pl.when((c >= 0) & (c < count))(functools.partial(fn, stage, c))
        send_raw(t + AHEAD)

        @pl.when(t == max(na + A_AT[5], nd + D_AT[5]))
        def _():
            mbuf[...] = mfull[...].T
            sbuf[...] = sfull[...].T
            send(mbuf.at[other_half], nmom_t.at[x], m_ss.at[0], m_rs.at[0], partner)
            send(sbuf.at[other_half], nswa_t.at[x], m_ss.at[0], m_rs.at[1], partner)
            pltpu.make_async_copy(mbuf.at[half], nmom_t.at[x], l_sem.at[5]).start()
            pltpu.make_async_copy(sbuf.at[half], nswa_t.at[x], l_sem.at[6]).start()

        return carry

    lax.fori_loop(0, max(na + A_AT[-1], nd + D_AT[-1]), slot, 0)
    pltpu.make_async_copy(mbuf.at[half], nmom_t.at[x], l_sem.at[5]).wait()
    pltpu.make_async_copy(sbuf.at[half], nswa_t.at[x], l_sem.at[6]).wait()
    drain(nmom_t.at[other], m_rs.at[0])
    drain(nswa_t.at[other], m_rs.at[1])
    drain(mbuf, m_ss.at[0])

    def wait_out(c, carry):
        @pl.when(c < na)
        def _():
            a_store(c, x).wait()
            a_store(c, other).wait()

        @pl.when(c < nd)
        def _():
            d_store(c).wait()

        return carry

    lax.fori_loop(0, max(na, nd), wait_out, 0)


def per_device(local, outer, momentum, swa, tokens, step_no):
    mats, rows, width = outer.shape
    na = rows // R // 2
    nd = rows // R - na
    f32, bf16, i32 = jnp.float32, jnp.bfloat16, jnp.int32
    vmem, dma = pltpu.VMEM, pltpu.SemaphoreType.DMA
    wide = NZ * LANES
    scratch = [
        vmem((na, NY - 1, mats, R, wide), bf16),
        vmem((mats, na * R, wide), bf16),
        vmem((mats, na * R, wide), bf16),
        vmem((na, NZ, mats, R, LANES), f32),
        vmem((na, 4, 2, mats, R, LANES), f32),
        vmem((na, mats, R, LANES), f32),
        vmem((na, R, LANES), f32),
        vmem((na, NY, NZ, R, LANES), bf16),
        vmem((na, NY, NZ, R, LANES), bf16),
        vmem((na, mats, R, width), bf16),
        vmem((nd, R, width), bf16),
        vmem((nd * R, width), bf16),
        vmem((nd * R, width), bf16),
        vmem((nd, NZ, NY, R, LANES), f32),
        vmem((nd, 4, 2, NY, R, LANES), f32),
        vmem((nd, NY, R, LANES), f32),
        vmem((nd, NY - 1, R, LANES), f32),
        vmem((nd, NY, NX, NZ, R, LANES), bf16),
        vmem((nd, mats, R, width), bf16),
        vmem((NY + 1, 8, LANES), i32),
        vmem((NZ, 8, LANES), i32),
        vmem((2, 8, LANES), i32),
        vmem((8, LANES), f32),
        vmem((LANES, rows), f32),
        vmem((LANES, rows), f32),
        vmem((rows, LANES), f32),
        vmem((rows, LANES), f32),
        vmem((rows, LANES), bf16),
        dma((2, 9)), dma((na, 9)), dma((2, 9)), dma((nd, 9)), dma((2, 4)),
        dma((3,)), dma((3,)), dma((1,)), dma((2,)), dma((7,)), dma((na + nd, 2)),
    ]
    anywhere = pl.BlockSpec(memory_space=pl.ANY)
    in_hbm = pl.BlockSpec(memory_space=pltpu.HBM)
    in_smem = pl.BlockSpec(memory_space=pltpu.SMEM)
    turned = jax.ShapeDtypeStruct((mats, LANES // 2, rows), f32)
    shapes = (jax.ShapeDtypeStruct(outer.shape, bf16), turned, turned)
    results = pl.pallas_call(
        functools.partial(kernel, na, nd, rows),
        out_shape=shapes,
        in_specs=[in_hbm] * 4 + [in_smem] * 2,
        out_specs=(anywhere,) * 3,
        scratch_shapes=scratch,
        compiler_params=pltpu.CompilerParams(
            collective_id=0, has_side_effects=True, vmem_limit_bytes=47 * 2**20
        ),
    )(local, outer, jnp.swapaxes(momentum, 1, 2), jnp.swapaxes(swa, 1, 2), tokens, step_no)
    new_weights, new_mom, new_swa = results
    return new_weights, jnp.swapaxes(new_mom, 1, 2), jnp.swapaxes(new_swa, 1, 2)


def solution(mesh):
    return jax.shard_map(
        per_device,
        mesh=mesh,
        in_specs=(
            P("rep", None, "fsdp", None),
            P(None, "fsdp", None),
            P(None, "fsdp", "rep"),
            P(None, "fsdp", "rep"),
            P("rep"),
            P(),
        ),
        out_specs=(P(None, "fsdp", None), P(None, "fsdp", "rep"), P(None, "fsdp", "rep")),
        check_vma=False,
    )
```

time: 573 us -> 93.7 us (0.16)
  waiting for transfers between devices: 492 us -> 0 us
  Pallas kernels: 0 us -> 86.2 us
  blocking collectives: 28.6 us -> 0 us
  other arithmetic: 15.6 us -> 0 us
  between operations: 16.1 us -> 1.94 us
  local copies, waits for them, and re-layouts: 19 us -> 5.13 us
    reduce_scatter x1 -> x0, waiting for transfers between devices: 368 us -> none  [reduce_terms(): return lax.psum_scatter(terms, 'rep', scatter_dimension=2, tiled=True)]
    all_gather x1 -> x0, waiting for transfers between devices: 124 us -> none  [per_device(): lax.all_gather(updated.astype(jnp.bfloat16), 'rep', axis=2, tiled=True)]
    pallas_call x0 -> x1, Pallas kernels: none -> 86.2 us  [per_device(): pl.pallas_call(functools.partial(kernel, na, nd, rows), out_shape=shapes,...]
    psum x1 -> x0, blocking collectives: 28.6 us -> none  [token_total(): summed = lax.psum(token_counts, 'rep')]
    unnamed x7, local copies, waits for them, and re-layouts: 19 us -> 5.13 us
    mul x1 -> x0, other arithmetic: 7.77 us -> none  [per_device(): pseudo_grad = reduce_terms(own_count / total * difference)]
    convert_element_type x1 -> x0, other arithmetic: 6.13 us -> none  [per_device(): outer = outer_weights.astype(jnp.float32)]
  transfers between devices with their start and end apart: 2 -> 0, of which waited for: 2 -> 0; matrix products, arithmetic and copies ran while one was open for 1% -> 0% of each run, Pallas kernels for 0% -> 0%
where the time goes in v2:
time: 93.7 us; the launch traced here: 93.3 us
  Pallas kernels  86.2 us (92%)
  local copies, waits for them, and re-layouts  5.13 us (5%)
  between operations  1.94 us (2%)
    pallas_call x1, Pallas kernels, per_device(): pl.pallas_call(functools.partial(kernel, na, nd, rows), out_shape=shapes,...  86.2 us
    unnamed x7, local copies, waits for them, and re-layouts  5.13 us

profile of v2, /device:TPU:2, one launch (start us, length us, event | category | flops | bytes accessed | tf_op | source)
XLA Modules:
  0.0 93.3 jit_solution(11328915294888277352)
XLA Ops:
  1.9 0.0 copy-start
  1.9 0.9 copy-done
  2.8 0.0 copy-start.1
  2.8 0.9 copy-done.1
  3.7 86.2 %shard_map.85 = (bf16[2,256,4096]{2,1,0:T(8,128)(2,1)S(1)}, f32[2,64,256]{2,1,0:T(8,128)S(1)}, f32[2,64,256]{2,1,0:T(8,128)S(1)}) custom-call(bf16[1,2,256,4096]{3,2,1,0:T(8,128)(2,1)} %local.1, bf16[2,256,4096]{2,1,0:T(8,128)(2,1)} %outer.1, f32[2,64,256]{2,1,0:T(8,128)S(1)} %bitcast.4, f32[2,64,256]{2,1,0:T(8,128)S(1)} %bitcast.5, s32[1]{0:T(128)S(6)} %copy.12.tokens, ...), custom_call_target="tpu_custom_call" | custom-call | tf_op jit(solution)/shard_map/pallas_call | solution.py:384
  90.0 2.0 %copy.14 = bf16[2,256,4096]{2,1,0:T(8,128)(2,1)} copy(bf16[2,256,4096]{2,1,0:T(8,128)(2,1)S(1)} %get-tuple-element.12) | data formatting | bytes 8388608
  92.0 0.7 copy.15
  92.6 0.7 copy.16
Async XLA Ops:
  1.9 0.9 copy-start
  2.8 0.9 copy-start.1

commit v3 on v2

--- a/solution.py
+++ b/solution.py
@@ -12,19 +12,25 @@
 LANES = 128
 R = 16
 AHEAD = 3
-A_AT = tuple(range(9))
-D_AT = tuple(range(9))
-ORDER = tuple((kind, stage) for stage in range(9) for kind in "AD")
+NB = 5
+ND = 7
+A_AT = (0, 1, 2, 3, 4, 5, 6, 8, 10)
+B_AT = (0, 1, 2, 3, 4, 5, 6, 8, 10, 12, 13, 14)
+D_AT = (0, 1, 2, 3, 4, 6, 7, 9, 10, 12)
+ORDER = (
+    ("B", 9), ("A", 0), ("A", 1), ("D", 0), ("A", 2), ("A", 3), ("A", 7), ("D", 7), ("A", 4), ("A", 5), ("D", 5), ("B", 8), ("B", 10), ("D", 9), ("A", 6), ("D", 1), ("B", 11), ("B", 5), ("B", 7), ("B", 6), ("A", 8), ("D", 2), ("D", 8), ("D", 6), ("D", 3), ("D", 4),
+)
+FLIGHT = 1 + max(b - a for at in (A_AT, B_AT, D_AT) for a, b in zip(at, at[1:]))
 RAW, RING, MID, FIRST, SECOND, LAST = 0, 1, 5, 6, 7, 8
 
 
 def kernel(
     na, nd, rows,
-    local, outer, mom_t, swa_t, tokens, step_no,
-    out, nmom_t, nswa_t,
-    a_raw, a_own, a_out, a_p, a_r, a_q, a_qx, a_w, a_wx, a_stage,
+    local, outer, mom_t, tokens,
+    out, grad_t, upd_t,
+    a_raw, a_own, a_out, a_p, a_r, a_q, a_qx, a_w, a_wx, b_w, a_stage,
     d_raw, d_own, d_out, d_p, d_r, d_q, d_qy, d_w, d_stage,
-    cnt, cnt_z, cnt_x, total, mbuf, sbuf, mfull, sfull, ofull,
+    cnt, cnt_z, cnt_x, total, gbuf, ubuf, mfull, gfull, ufull, ofull,
     a_ss, a_rs, d_ss, d_rs, raw_ss, c_ss, c_rs, m_ss, m_rs, l_sem, o_sem,
 ):
     f32, bf16 = jnp.float32, jnp.bfloat16
@@ -79,8 +85,7 @@
     ]
     late_loads = [
         pltpu.make_async_copy(outer.at[x, :, cols], ofull, l_sem.at[0]),
-        pltpu.make_async_copy(mom_t.at[x], mbuf.at[half], l_sem.at[5]),
-        pltpu.make_async_copy(swa_t.at[x], sbuf.at[half], l_sem.at[6]),
+        pltpu.make_async_copy(mom_t.at[x], gbuf.at[half], l_sem.at[5]),
     ]
     for load in loads + late_loads:
         load.start()
@@ -110,9 +115,9 @@
         up, down = at(y, z + sign, x), at(y, z - sign, x)
 
         def step(k, long, short):
-            send(long, r.at[c, k, 0], ss.at[c % 2, RING + k], rs.at[c, RING + k], up)
+            send(long, r.at[c, k, 0], ss.at[c % FLIGHT, RING + k], rs.at[c, RING + k], up)
             if k < 3:
-                send(short, r.at[c, k, 1], ss.at[c % 2, RING + k], rs.at[c, RING + k], down)
+                send(short, r.at[c, k, 1], ss.at[c % FLIGHT, RING + k], rs.at[c, RING + k], down)
 
         if stage == 0:
             step(0, p.at[c, zi(4 * sign)], p.at[c, zi(-3 * sign)])
@@ -125,17 +130,14 @@
             if k < 2:
                 r[c, k, 1] += p[c, zi(-(2 - k) * sign)]
             step(k + 1, r.at[c, k, 0], r.at[c, k, 1])
-        drain(came, ss.at[c % 2, RING + k])
+        drain(came, ss.at[c % FLIGHT, RING + k])
 
     def update(rws, pg_sum):
         o = ofull[rws, :].astype(f32)
         pg = pg_sum / total[0:1, :]
-        nm = 0.9 * mfull[rws, :] + pg
-        upd = o - 0.7 * (pg + 0.9 * nm)
-        s = sfull[rws, :]
-        divisor = step_no[0].astype(f32) + 1.0
-        mfull[rws, :] = nm
-        sfull[rws, :] = s + (upd - s) / divisor
+        upd = o - 0.7 * (pg + 0.9 * (0.9 * mfull[rws, :] + pg))
+        gfull[rws, :] = pg
+        ufull[rws, :] = upd
         return upd.astype(bf16)
 
     def a_store(c, m):
@@ -145,13 +147,13 @@
         ring = functools.partial(ring_stage, c=c, sign=1 - 2 * (c % 2), p=a_p, r=a_r, ss=a_ss, rs=a_rs)
 
         def sems(k):
-            return a_ss.at[c % 2, k], a_rs.at[c, k]
+            return a_ss.at[c % FLIGHT, k], a_rs.at[c, k]
 
         def landed(ref, k):
             drain(ref, a_rs.at[c, k])
 
         def left(ref, k):
-            drain(ref, a_ss.at[c % 2, k])
+            drain(ref, a_ss.at[c % FLIGHT, k])
 
         if stage == 0:
             landed(a_raw.at[c], RAW)
@@ -199,6 +201,56 @@
             a_store(c, other).start()
             left(a_wx.at[c], LAST)
 
+    def b_stage_fn(stage, c):
+        sign = 1 - 2 * (c % 2)
+        up, down = at(y, z + sign, x), at(y, z - sign, x)
+
+        def sems(k):
+            return a_ss.at[c % FLIGHT, k], a_rs.at[c, k]
+
+        def landed(ref, k):
+            drain(ref, a_rs.at[c, k])
+
+        def left(ref, k):
+            drain(ref, a_ss.at[c % FLIGHT, k])
+
+        def step(k):
+            long, short = b_w.at[c, zi(-k * sign)], b_w.at[c, zi(k * sign)]
+            send(long, long, *sems(LAST + k), up)
+            if k < 3:
+                send(short, short, *sems(LAST + k), down)
+
+        if stage == 5:
+            landed(a_qx.at[c], MID)
+            mine = b_w.at[c, z, y, x]
+            mine[...] = update(a_rows(c), a_q[c, x] + a_qx[c])
+            send(mine, mine, *sems(FIRST), partner)
+            left(a_qx.at[c], MID)
+        elif stage == 6:
+            landed(b_w.at[c, z, y, other], FIRST)
+            mine = b_w.at[c, z, y]
+            for k in (2, 1, 3):
+                send(mine, mine, *sems(SECOND), y_peers[k - 1])
+            left(b_w.at[c, z, y, other], FIRST)
+        elif stage == 7:
+            landed(b_w.at[c, z, pl.ds(0, NY - 1)], SECOND)
+            step(0)
+            left(b_w.at[c, z, pl.ds(0, NY - 1)], SECOND)
+        else:
+            k = stage - 8
+            came = b_w.at[c, pl.ds(0, 2 if k < 3 else 1)]
+            landed(came, LAST + k)
+            if k < 3:
+                step(k + 1)
+            else:
+                for yy in range(NY):
+                    for zz in range(NZ):
+                        for m in range(2):
+                            a_stage[c, m, :, lanes(yy * NZ + zz)] = b_w[c, zz, yy, m]
+                for m in range(2):
+                    a_store(c, m).start()
+            left(came, LAST + k)
+
     def d_store(c):
         return pltpu.make_async_copy(d_stage.at[c], out.at[:, d_rows(c), :], o_sem.at[na + c, 0])
 
@@ -206,13 +258,13 @@
         ring = functools.partial(ring_stage, c=c, sign=2 * (c % 2) - 1, p=d_p, r=d_r, ss=d_ss, rs=d_rs)
 
         def sems(k):
-            return d_ss.at[c % 2, k], d_rs.at[c, k]
+            return d_ss.at[c % FLIGHT, k], d_rs.at[c, k]
 
         def landed(ref, k):
             drain(ref, d_rs.at[c, k])
 
         def left(ref, k):
-            drain(ref, d_ss.at[c % 2, k])
+            drain(ref, d_ss.at[c % FLIGHT, k])
 
         if stage == 0:
             landed(d_raw.at[c], RAW)
@@ -247,25 +299,30 @@
         elif stage == 7:
             landed(d_w.at[c, y, other], SECOND)
             mine = d_w.at[c, y]
-            for k in (2, 1, 3):
+            for k in (1, 3):
                 send(mine, mine, *sems(LAST), y_peers[k - 1])
             left(d_w.at[c, y, x], SECOND)
+        elif stage == 8:
+            landed(d_w.at[c, pl.ds(0, 2)], LAST)
+            for k, m in ((1, 0), (-1, 1)):
+                theirs = d_w.at[c, yi(-k), m]
+                send(theirs, theirs, *sems(LAST + 1), at(y + k, z, x))
+            left(d_w.at[c, pl.ds(0, 2)], LAST)
         else:
-            landed(d_w.at[c, pl.ds(0, NY - 1)], LAST)
+            landed(d_w.at[c, 0], LAST + 1)
             for yy in range(NY):
                 for zz in range(NZ):
                     for m in range(2):
                         d_stage[c, m, :, lanes(yy * NZ + zz)] = d_w[c, yy, m, zz]
             d_store(c).start()
-            left(d_w.at[c, pl.ds(0, NY - 1)], LAST)
+            left(d_w.at[c, 0], LAST + 1)
 
     for k in range(1, NY):
         send(cnt.at[0], cnt.at[k], c_ss.at[0], c_rs.at[0], y_peers[k - 1])
     send(cnt.at[0], cnt.at[NY], c_ss.at[0], c_rs.at[0], partner)
     for c in range(AHEAD):
         send_raw(c)
-    send(mom_t.at[other], mbuf.at[half], m_ss.at[0], m_rs.at[0], partner)
-    send(swa_t.at[other], sbuf.at[half], m_ss.at[0], m_rs.at[1], partner)
+    send(mom_t.at[other], gbuf.at[half], m_ss.at[0], m_rs.at[0], partner)
     drain(cnt.at[pl.ds(0, NY)], c_rs.at[0])
     drain(cnt.at[pl.ds(0, NY)], c_ss.at[0])
     cnt_z[0] = cnt[0] + cnt[1] + cnt[2] + cnt[3]
@@ -290,37 +347,40 @@
             drain(cnt_x.at[0], c_rs.at[2])
             drain(cnt_x.at[0], c_ss.at[2])
             total[...] = (cnt_x[0] + cnt_x[1]).astype(f32)
-            drain(mbuf.at[other_half], m_rs.at[0])
-            drain(sbuf.at[other_half], m_rs.at[1])
-            drain(mbuf, m_ss.at[0])
+            drain(gbuf.at[other_half], m_rs.at[0])
+            drain(gbuf.at[other_half], m_ss.at[0])
             for load in late_loads:
                 load.wait()
-            mfull[...] = mbuf[...].T
-            sfull[...] = sbuf[...].T
+            mfull[...] = gbuf[...].T
 
         for kind, stage in ORDER:
-            first, count, fn = (A_AT, na, a_stage_fn) if kind == "A" else (D_AT, nd, d_stage_fn)
-            c = t - first[stage]
-            pl.when((c >= 0) & (c < count))(functools.partial(fn, stage, c))
+            if kind == "D":
+                c, low, high, fn = t - D_AT[stage], 0, nd, d_stage_fn
+            elif kind == "B":
+                c, low, high, fn = t - B_AT[stage], 0, NB, b_stage_fn
+            else:
+                c, low, high, fn = t - A_AT[stage], NB if stage > 4 else 0, na, a_stage_fn
+            pl.when((c >= low) & (c < high))(functools.partial(fn, stage, c))
         send_raw(t + AHEAD)
 
-        @pl.when(t == max(na + A_AT[5], nd + D_AT[5]))
-        def _():
-            mbuf[...] = mfull[...].T
-            sbuf[...] = sfull[...].T
-            send(mbuf.at[other_half], nmom_t.at[x], m_ss.at[0], m_rs.at[0], partner)
-            send(sbuf.at[other_half], nswa_t.at[x], m_ss.at[0], m_rs.at[1], partner)
-            pltpu.make_async_copy(mbuf.at[half], nmom_t.at[x], l_sem.at[5]).start()
-            pltpu.make_async_copy(sbuf.at[half], nswa_t.at[x], l_sem.at[6]).start()
+        @pl.when(t == max(na + A_AT[5], NB + B_AT[5], nd + D_AT[5]))
+        def _():
+            gbuf[...] = gfull[...].T
+            ubuf[...] = ufull[...].T
+            send(gbuf.at[other_half], grad_t.at[x], m_ss.at[0], m_rs.at[0], partner)
+            send(ubuf.at[other_half], upd_t.at[x], m_ss.at[1], m_rs.at[1], partner)
+            pltpu.make_async_copy(gbuf.at[half], grad_t.at[x], l_sem.at[5]).start()
+            pltpu.make_async_copy(ubuf.at[half], upd_t.at[x], l_sem.at[6]).start()
 
         return carry
 
-    lax.fori_loop(0, max(na + A_AT[-1], nd + D_AT[-1]), slot, 0)
-    pltpu.make_async_copy(mbuf.at[half], nmom_t.at[x], l_sem.at[5]).wait()
-    pltpu.make_async_copy(sbuf.at[half], nswa_t.at[x], l_sem.at[6]).wait()
-    drain(nmom_t.at[other], m_rs.at[0])
-    drain(nswa_t.at[other], m_rs.at[1])
-    drain(mbuf, m_ss.at[0])
+    lax.fori_loop(0, max(na + A_AT[-1], NB + B_AT[-1], nd + D_AT[-1]), slot, 0)
+    pltpu.make_async_copy(gbuf.at[half], grad_t.at[x], l_sem.at[5]).wait()
+    pltpu.make_async_copy(ubuf.at[half], upd_t.at[x], l_sem.at[6]).wait()
+    drain(grad_t.at[other], m_rs.at[0])
+    drain(upd_t.at[other], m_rs.at[1])
+    drain(gbuf.at[other_half], m_ss.at[0])
+    drain(ubuf.at[other_half], m_ss.at[1])
 
     def wait_out(c, carry):
         @pl.when(c < na)
@@ -339,8 +399,8 @@
 
 def per_device(local, outer, momentum, swa, tokens, step_no):
     mats, rows, width = outer.shape
-    na = rows // R // 2
-    nd = rows // R - na
+    nd = ND
+    na = rows // R - nd
     f32, bf16, i32 = jnp.float32, jnp.bfloat16, jnp.int32
     vmem, dma = pltpu.VMEM, pltpu.SemaphoreType.DMA
     wide = NZ * LANES
@@ -354,6 +414,7 @@
         vmem((na, R, LANES), f32),
         vmem((na, NY, NZ, R, LANES), bf16),
         vmem((na, NY, NZ, R, LANES), bf16),
+        vmem((NB, NZ, NY, NX, R, LANES), bf16),
         vmem((na, mats, R, width), bf16),
         vmem((nd, R, width), bf16),
         vmem((nd * R, width), bf16),
@@ -372,9 +433,10 @@
         vmem((LANES, rows), f32),
         vmem((rows, LANES), f32),
         vmem((rows, LANES), f32),
+        vmem((rows, LANES), f32),
         vmem((rows, LANES), bf16),
-        dma((2, 9)), dma((na, 9)), dma((2, 9)), dma((nd, 9)), dma((2, 4)),
-        dma((3,)), dma((3,)), dma((1,)), dma((2,)), dma((7,)), dma((na + nd, 2)),
+        dma((FLIGHT, 12)), dma((na, 12)), dma((FLIGHT, 10)), dma((nd, 10)), dma((2, 4)),
+        dma((3,)), dma((3,)), dma((2,)), dma((2,)), dma((7,)), dma((na + nd, 2)),
     ]
     anywhere = pl.BlockSpec(memory_space=pl.ANY)
     in_hbm = pl.BlockSpec(memory_space=pltpu.HBM)
@@ -384,15 +446,17 @@
     results = pl.pallas_call(
         functools.partial(kernel, na, nd, rows),
         out_shape=shapes,
-        in_specs=[in_hbm] * 4 + [in_smem] * 2,
+        in_specs=[in_hbm] * 3 + [in_smem],
         out_specs=(anywhere,) * 3,
         scratch_shapes=scratch,
         compiler_params=pltpu.CompilerParams(
             collective_id=0, has_side_effects=True, vmem_limit_bytes=47 * 2**20
         ),
-    )(local, outer, jnp.swapaxes(momentum, 1, 2), jnp.swapaxes(swa, 1, 2), tokens, step_no)
-    new_weights, new_mom, new_swa = results
-    return new_weights, jnp.swapaxes(new_mom, 1, 2), jnp.swapaxes(new_swa, 1, 2)
+    )(local, outer, jnp.swapaxes(momentum, 1, 2), tokens)
+    new_weights, grad, updated = results
+    grad, updated = jnp.swapaxes(grad, 1, 2), jnp.swapaxes(updated, 1, 2)
+    divisor = step_no[0].astype(f32) + 1.0
+    return new_weights, 0.9 * momentum + grad, swa + (updated - swa) / divisor
 
 
 def solution(mesh):

time: 93.7 us -> 86.1 us (0.919)
  Pallas kernels: 86.2 us -> 80.3 us
  local copies, waits for them, and re-layouts: 5.13 us -> 2.91 us
    pallas_call x1, Pallas kernels: 86.2 us -> 80.3 us  [per_device(): pl.pallas_call(functools.partial(kernel, na, nd, rows), out_shape=shapes,...]
    unnamed x7 -> x5, local copies, waits for them, and re-layouts: 5.13 us -> 2.91 us
where the time goes in v3:
time: 86.1 us; the launch traced here: 85.9 us
  Pallas kernels  80.3 us (93%)
  local copies, waits for them, and re-layouts  2.91 us (3%)
  between operations  1.95 us (2%)
    pallas_call x1, Pallas kernels, per_device(): pl.pallas_call(functools.partial(kernel, na, nd, rows), out_shape=shapes,...  80.3 us
    unnamed x5, local copies, waits for them, and re-layouts  2.91 us

profile of v3, /device:TPU:2, one launch (start us, length us, event | category | flops | bytes accessed | tf_op | source)
XLA Modules:
  0.0 85.9 jit_solution(12701519919710919012)
XLA Ops:
  1.3 0.0 copy-start
  1.3 0.9 %copy-done = f32[2,256,64]{1,2,0:T(8,128)S(1)} copy-done((f32[2,256,64]{1,2,0:T(8,128)S(1)}, f32[2,256,64]{1,2,0:T(8,128)}, u32[]{:S(2)}) %copy-start) | copy-done | bytes 131096
  2.2 0.0 copy-start.1
  2.2 80.3 %shard_map.85 = (bf16[2,256,4096]{2,1,0:T(8,128)(2,1)S(1)}, f32[2,64,256]{2,1,0:T(8,128)S(1)}, f32[2,64,256]{2,1,0:T(8,128)S(1)}) custom-call(bf16[1,2,256,4096]{3,2,1,0:T(8,128)(2,1)} %local.1, bf16[2,256,4096]{2,1,0:T(8,128)(2,1)} %outer.1, f32[2,64,256]{2,1,0:T(8,128)S(1)} %bitcast.10, s32[1]{0:T(128)S(6)} %copy.10.tokens), custom_call_target="tpu_custom_call" | custom-call | tf_op jit(solution)/shard_map/pallas_call | solution.py:446
  83.1 0.0 copy-done.1
  83.1 0.7 fusion.1
  83.9 2.0 %copy.12 = bf16[2,256,4096]{2,1,0:T(8,128)(2,1)} copy(bf16[2,256,4096]{2,1,0:T(8,128)(2,1)S(1)} %get-tuple-element.14) | data formatting | bytes 8388608
Async XLA Ops:
  1.3 0.9 %copy-start = (f32[2,256,64]{1,2,0:T(8,128)S(1)}, f32[2,256,64]{1,2,0:T(8,128)}, u32[]{:S(2)}) copy-start(f32[2,256,64]{1,2,0:T(8,128)} %param.8) | copy-start | bytes 393220
  2.2 81.0 %copy-start.1 = (f32[2,256,64]{1,2,0:T(8,128)S(1)}, f32[2,256,64]{1,2,0:T(8,128)}, u32[]{:S(2)}) copy-start(f32[2,256,64]{1,2,0:T(8,128)} %param.9) | copy-start | bytes 393220

commit v4 on v3

--- a/solution.py
+++ b/solution.py
@@ -14,13 +14,12 @@
 AHEAD = 3
 NB = 5
 ND = 7
-A_AT = (0, 1, 2, 3, 4, 5, 6, 8, 10)
+A_AT = (0, 1, 2, 3, 4, 5, 6, 8)
 B_AT = (0, 1, 2, 3, 4, 5, 6, 8, 10, 12, 13, 14)
-D_AT = (0, 1, 2, 3, 4, 6, 7, 9, 10, 12)
+D_AT = (0, 1, 2, 3, 4, 6, 7, 9, 10)
 ORDER = (
-    ("B", 9), ("A", 0), ("A", 1), ("D", 0), ("A", 2), ("A", 3), ("A", 7), ("D", 7), ("A", 4), ("A", 5), ("D", 5), ("B", 8), ("B", 10), ("D", 9), ("A", 6), ("D", 1), ("B", 11), ("B", 5), ("B", 7), ("B", 6), ("A", 8), ("D", 2), ("D", 8), ("D", 6), ("D", 3), ("D", 4),
+    ("B", 9), ("A", 0), ("A", 1), ("D", 0), ("A", 2), ("A", 3), ("A", 7), ("D", 7), ("A", 4), ("A", 5), ("D", 5), ("B", 8), ("B", 10), ("A", 6), ("D", 1), ("B", 11), ("B", 5), ("B", 7), ("B", 6), ("D", 2), ("D", 8), ("D", 6), ("D", 3), ("D", 4),
 )
-FLIGHT = 1 + max(b - a for at in (A_AT, B_AT, D_AT) for a, b in zip(at, at[1:]))
 RAW, RING, MID, FIRST, SECOND, LAST = 0, 1, 5, 6, 7, 8
 
 
@@ -28,10 +27,10 @@
     na, nd, rows,
     local, outer, mom_t, tokens,
     out, grad_t, upd_t,
-    a_raw, a_own, a_out, a_p, a_r, a_q, a_qx, a_w, a_wx, b_w, a_stage,
-    d_raw, d_own, d_out, d_p, d_r, d_q, d_qy, d_w, d_stage,
+    a_raw, a_own, a_out, a_p, a_r, a_q, a_qx, a_v, b_w, b_stage,
+    d_raw, d_own, d_out, d_p, d_r, d_q, d_qy, d_v,
     cnt, cnt_z, cnt_x, total, gbuf, ubuf, mfull, gfull, ufull, ofull,
-    a_ss, a_rs, d_ss, d_rs, raw_ss, c_ss, c_rs, m_ss, m_rs, l_sem, o_sem,
+    a_ss, b_ss, a_rs, d_ss, d_rs, c_ss, c_rs, m_ss, m_rs, l_sem, o_sem, v_sem, end_s,
 ):
     f32, bf16 = jnp.float32, jnp.bfloat16
     rep, fsdp = lax.axis_index("rep"), lax.axis_index("fsdp")
@@ -104,20 +103,20 @@
                 theirs = pl.ds(pl.multiple_of(yi(k) * (NZ * LANES), NZ * LANES), NZ * LANES)
                 send(
                     local.at[0, :, a_rows(c), theirs], a_raw.at[c, k - 1],
-                    raw_ss.at[0, c % 4], a_rs.at[c, RAW], y_peers[k - 1],
+                    a_ss.at[RAW], a_rs.at[c, RAW], y_peers[k - 1],
                 )
 
         @pl.when(c < nd)
         def _():
-            send(local.at[0, other, d_rows(c), :], d_raw.at[c], raw_ss.at[1, c % 4], d_rs.at[c, RAW], partner)
+            send(local.at[0, other, d_rows(c), :], d_raw.at[c], d_ss.at[RAW], d_rs.at[c, RAW], partner)
 
     def ring_stage(stage, c, sign, p, r, ss, rs):
         up, down = at(y, z + sign, x), at(y, z - sign, x)
 
         def step(k, long, short):
-            send(long, r.at[c, k, 0], ss.at[c % FLIGHT, RING + k], rs.at[c, RING + k], up)
+            send(long, r.at[c, k, 0], ss.at[RING + k], rs.at[c, RING + k], up)
             if k < 3:
-                send(short, r.at[c, k, 1], ss.at[c % FLIGHT, RING + k], rs.at[c, RING + k], down)
+                send(short, r.at[c, k, 1], ss.at[RING + k], rs.at[c, RING + k], down)
 
         if stage == 0:
             step(0, p.at[c, zi(4 * sign)], p.at[c, zi(-3 * sign)])
@@ -130,7 +129,6 @@
             if k < 2:
                 r[c, k, 1] += p[c, zi(-(2 - k) * sign)]
             step(k + 1, r.at[c, k, 0], r.at[c, k, 1])
-        drain(came, ss.at[c % FLIGHT, RING + k])
 
     def update(rws, pg_sum):
         o = ofull[rws, :].astype(f32)
@@ -140,20 +138,14 @@
         ufull[rws, :] = upd
         return upd.astype(bf16)
 
-    def a_store(c, m):
-        return pltpu.make_async_copy(a_stage.at[c, m], out.at[m, a_rows(c), :], o_sem.at[c, m])
-
     def a_stage_fn(stage, c):
         ring = functools.partial(ring_stage, c=c, sign=1 - 2 * (c % 2), p=a_p, r=a_r, ss=a_ss, rs=a_rs)
 
         def sems(k):
-            return a_ss.at[c % FLIGHT, k], a_rs.at[c, k]
+            return a_ss.at[k], a_rs.at[c, k]
 
         def landed(ref, k):
             drain(ref, a_rs.at[c, k])
-
-        def left(ref, k):
-            drain(ref, a_ss.at[c % FLIGHT, k])
 
         if stage == 0:
             landed(a_raw.at[c], RAW)
@@ -165,7 +157,6 @@
                         acc += cnt_f(k) * (o - a_raw[c, k - 1, m, :, lanes(zz)].astype(f32))
                     a_p[c, zz, m] = acc
             ring(0)
-            drain(a_raw.at[c], raw_ss.at[0, c % 4])
         elif stage <= 3:
             ring(stage)
         elif stage == 4:
@@ -174,45 +165,31 @@
             send(a_q.at[c, other], a_qx.at[c], *sems(MID), partner)
         elif stage == 5:
             landed(a_qx.at[c], MID)
-            mine = a_w.at[c, y, z]
-            mine[...] = update(a_rows(c), a_q[c, x] + a_qx[c])
+            a_v[c] = update(a_rows(c), a_q[c, x] + a_qx[c])
+            place = out.at[x, a_rows(c), cols]
+            pltpu.make_async_copy(a_v.at[c], place, v_sem.at[0, c % 4]).start()
             for k in (4, 3, 5, 2, 6, 1, 7):
-                send(mine, mine, *sems(FIRST), z_peers[k - 1])
-            left(a_qx.at[c], MID)
+                send(a_v.at[c], place, *sems(FIRST), z_peers[k - 1])
         elif stage == 6:
-            landed(a_w.at[c, y, pl.ds(0, NZ - 1)], FIRST)
-            mine = a_w.at[c, y]
+            landed(out.at[x, a_rows(c), pl.ds(0, (NZ - 1) * LANES)], FIRST)
+            drain(a_v.at[c], v_sem.at[0, c % 4])
+            place = out.at[x, a_rows(c), ycols]
             for k in (2, 1, 3):
-                send(mine, mine, *sems(SECOND), y_peers[k - 1])
-            left(a_w.at[c, y, pl.ds(0, NZ - 1)], FIRST)
-        elif stage == 7:
-            landed(a_w.at[c, pl.ds(0, NY - 1)], SECOND)
-            send(a_w.at[c], a_wx.at[c], *sems(LAST), partner)
-            for yy in range(NY):
-                for zz in range(NZ):
-                    a_stage[c, x, :, lanes(yy * NZ + zz)] = a_w[c, yy, zz]
-            a_store(c, x).start()
-            left(a_w.at[c, pl.ds(0, NY - 1)], SECOND)
+                send(place, place, *sems(SECOND), y_peers[k - 1])
         else:
-            landed(a_wx.at[c], LAST)
-            for yy in range(NY):
-                for zz in range(NZ):
-                    a_stage[c, other, :, lanes(yy * NZ + zz)] = a_wx[c, yy, zz]
-            a_store(c, other).start()
-            left(a_wx.at[c], LAST)
+            landed(out.at[x, a_rows(c), pl.ds(0, (NY - 1) * NZ * LANES)], SECOND)
+            place = out.at[x, a_rows(c), :]
+            send(place, place, a_ss.at[LAST], end_s.at[0], partner)
 
     def b_stage_fn(stage, c):
         sign = 1 - 2 * (c % 2)
         up, down = at(y, z + sign, x), at(y, z - sign, x)
 
         def sems(k):
-            return a_ss.at[c % FLIGHT, k], a_rs.at[c, k]
+            return b_ss.at[k], a_rs.at[c, k]
 
         def landed(ref, k):
             drain(ref, a_rs.at[c, k])
-
-        def left(ref, k):
-            drain(ref, a_ss.at[c % FLIGHT, k])
 
         def step(k):
             long, short = b_w.at[c, zi(-k * sign)], b_w.at[c, zi(k * sign)]
@@ -225,17 +202,14 @@
             mine = b_w.at[c, z, y, x]
             mine[...] = update(a_rows(c), a_q[c, x] + a_qx[c])
             send(mine, mine, *sems(FIRST), partner)
-            left(a_qx.at[c], MID)
         elif stage == 6:
             landed(b_w.at[c, z, y, other], FIRST)
             mine = b_w.at[c, z, y]
             for k in (2, 1, 3):
                 send(mine, mine, *sems(SECOND), y_peers[k - 1])
-            left(b_w.at[c, z, y, other], FIRST)
         elif stage == 7:
             landed(b_w.at[c, z, pl.ds(0, NY - 1)], SECOND)
             step(0)
-            left(b_w.at[c, z, pl.ds(0, NY - 1)], SECOND)
         else:
             k = stage - 8
             came = b_w.at[c, pl.ds(0, 2 if k < 3 else 1)]
@@ -246,25 +220,17 @@
                 for yy in range(NY):
                     for zz in range(NZ):
                         for m in range(2):
-                            a_stage[c, m, :, lanes(yy * NZ + zz)] = b_w[c, zz, yy, m]
-                for m in range(2):
-                    a_store(c, m).start()
-            left(came, LAST + k)
-
-    def d_store(c):
-        return pltpu.make_async_copy(d_stage.at[c], out.at[:, d_rows(c), :], o_sem.at[na + c, 0])
+                            b_stage[c, m, :, lanes(yy * NZ + zz)] = b_w[c, zz, yy, m]
+                pltpu.make_async_copy(b_stage.at[c], out.at[:, a_rows(c), :], o_sem).start()
 
     def d_stage_fn(stage, c):
         ring = functools.partial(ring_stage, c=c, sign=2 * (c % 2) - 1, p=d_p, r=d_r, ss=d_ss, rs=d_rs)
 
         def sems(k):
-            return d_ss.at[c % FLIGHT, k], d_rs.at[c, k]
+            return d_ss.at[k], d_rs.at[c, k]
 
         def landed(ref, k):
             drain(ref, d_rs.at[c, k])
-
-        def left(ref, k):
-            drain(ref, d_ss.at[c % FLIGHT, k])
 
         if stage == 0:
             landed(d_raw.at[c], RAW)
@@ -276,7 +242,6 @@
                     mine = cnt_f(0) * (o - d_own[own, sl].astype(f32))
                     d_p[c, zz, yy] = mine + cnt_f(NY) * (o - d_raw[c, :, sl].astype(f32))
             ring(0)
-            drain(d_raw.at[c], raw_ss.at[1, c % 4])
         elif stage <= 3:
             ring(stage)
         elif stage == 4:
@@ -286,43 +251,34 @@
                 send(d_q.at[c, yi(k)], d_qy.at[c, k - 1], *sems(MID), y_peers[k - 1])
         elif stage == 5:
             landed(d_qy.at[c], MID)
-            mine = d_w.at[c, y, x, z]
-            mine[...] = update(d_rows(c), d_q[c, y] + d_qy[c, 0] + d_qy[c, 1] + d_qy[c, 2])
+            d_v[c] = update(d_rows(c), d_q[c, y] + d_qy[c, 0] + d_qy[c, 1] + d_qy[c, 2])
+            place = out.at[x, d_rows(c), cols]
+            pltpu.make_async_copy(d_v.at[c], place, v_sem.at[1, c % 4]).start()
             for k in (4, 3, 5, 2, 6, 1, 7):
-                send(mine, mine, *sems(FIRST), z_peers[k - 1])
-            left(d_qy.at[c], MID)
+                send(d_v.at[c], place, *sems(FIRST), z_peers[k - 1])
         elif stage == 6:
-            landed(d_w.at[c, y, x, pl.ds(0, NZ - 1)], FIRST)
-            mine = d_w.at[c, y, x]
-            send(mine, mine, *sems(SECOND), partner)
-            left(d_w.at[c, y, x, pl.ds(0, NZ - 1)], FIRST)
+            landed(out.at[x, d_rows(c), pl.ds(0, (NZ - 1) * LANES)], FIRST)
+            drain(d_v.at[c], v_sem.at[1, c % 4])
+            place = out.at[x, d_rows(c), ycols]
+            send(place, place, *sems(SECOND), partner)
         elif stage == 7:
-            landed(d_w.at[c, y, other], SECOND)
-            mine = d_w.at[c, y]
+            landed(out.at[other, d_rows(c), ycols], SECOND)
+            place = out.at[:, d_rows(c), ycols]
             for k in (1, 3):
-                send(mine, mine, *sems(LAST), y_peers[k - 1])
-            left(d_w.at[c, y, x], SECOND)
-        elif stage == 8:
-            landed(d_w.at[c, pl.ds(0, 2)], LAST)
+                send(place, place, *sems(LAST), y_peers[k - 1])
+        else:
+            landed(out.at[:, d_rows(c), pl.ds(0, 2 * NZ * LANES)], LAST)
             for k, m in ((1, 0), (-1, 1)):
-                theirs = d_w.at[c, yi(-k), m]
-                send(theirs, theirs, *sems(LAST + 1), at(y + k, z, x))
-            left(d_w.at[c, pl.ds(0, 2)], LAST)
-        else:
-            landed(d_w.at[c, 0], LAST + 1)
-            for yy in range(NY):
-                for zz in range(NZ):
-                    for m in range(2):
-                        d_stage[c, m, :, lanes(yy * NZ + zz)] = d_w[c, yy, m, zz]
-            d_store(c).start()
-            left(d_w.at[c, 0], LAST + 1)
-
+                theirs = pl.ds(pl.multiple_of(yi(-k) * (NZ * LANES), NZ * LANES), NZ * LANES)
+                place = out.at[m, d_rows(c), theirs]
+                send(place, place, d_ss.at[LAST + 1], end_s.at[1], at(y + k, z, x))
+
+    send_raw(0)
     for k in range(1, NY):
         send(cnt.at[0], cnt.at[k], c_ss.at[0], c_rs.at[0], y_peers[k - 1])
     send(cnt.at[0], cnt.at[NY], c_ss.at[0], c_rs.at[0], partner)
-    for c in range(AHEAD):
+    for c in range(1, AHEAD):
         send_raw(c)
-    send(mom_t.at[other], gbuf.at[half], m_ss.at[0], m_rs.at[0], partner)
     drain(cnt.at[pl.ds(0, NY)], c_rs.at[0])
     drain(cnt.at[pl.ds(0, NY)], c_ss.at[0])
     cnt_z[0] = cnt[0] + cnt[1] + cnt[2] + cnt[3]
@@ -341,8 +297,9 @@
                 acc += cnt_z[k]
             cnt_x[0] = acc
             send(cnt_x.at[0], cnt_x.at[1], c_ss.at[2], c_rs.at[2], partner)
-
-        @pl.when(t == 4)
+            send(mom_t.at[other], gbuf.at[half], m_ss.at[0], m_rs.at[0], partner)
+
+        @pl.when(t == 5)
         def _():
             drain(cnt_x.at[0], c_rs.at[2])
             drain(cnt_x.at[0], c_ss.at[2])
@@ -382,19 +339,25 @@
     drain(gbuf.at[other_half], m_ss.at[0])
     drain(ubuf.at[other_half], m_ss.at[1])
 
-    def wait_out(c, carry):
-        @pl.when(c < na)
-        def _():
-            a_store(c, x).wait()
-            a_store(c, other).wait()
-
-        @pl.when(c < nd)
-        def _():
-            d_store(c).wait()
-
-        return carry
-
-    lax.fori_loop(0, max(na, nd), wait_out, 0)
+    def part(mats, chunks, blocks):
+        return out.at[pl.ds(0, mats), pl.ds(0, chunks * R), pl.ds(0, blocks * LANES)]
+
+    for ref, sem in [
+        (part(1, na - NB, NY * NZ), end_s.at[0]), (part(1, nd, 2 * NZ), end_s.at[1]), (part(2, NB, NY * NZ), o_sem),
+        (a_raw, a_ss.at[RAW]), (a_r.at[:, 3, 0], a_ss.at[RING + 3]), (a_qx, a_ss.at[MID]),
+        (part(1, na - NB, NZ - 1), a_ss.at[FIRST]), (part(1, na - NB, (NY - 1) * NZ), a_ss.at[SECOND]),
+        (part(1, na - NB, NY * NZ), a_ss.at[LAST]),
+        (b_w.at[:, 0, 0, 0], b_ss.at[FIRST]), (b_w.at[:, 0, pl.ds(0, NY - 1)], b_ss.at[SECOND]),
+        (b_w.at[:, 0], b_ss.at[LAST + 3]),
+        (d_raw, d_ss.at[RAW]), (d_r.at[:, 3, 0], d_ss.at[RING + 3]), (d_qy, d_ss.at[MID]),
+        (part(1, nd, NZ - 1), d_ss.at[FIRST]), (part(1, nd, NZ), d_ss.at[SECOND]),
+        (part(2, nd, 2 * NZ), d_ss.at[LAST]), (part(1, nd, 2 * NZ), d_ss.at[LAST + 1]),
+    ]:
+        drain(ref, sem)
+    for k in range(3):
+        drain(a_r.at[:, k], a_ss.at[RING + k])
+        drain(b_w.at[:, pl.ds(0, 2)], b_ss.at[LAST + k])
+        drain(d_r.at[:, k], d_ss.at[RING + k])
 
 
 def per_device(local, outer, momentum, swa, tokens, step_no):
@@ -412,10 +375,9 @@
         vmem((na, 4, 2, mats, R, LANES), f32),
         vmem((na, mats, R, LANES), f32),
         vmem((na, R, LANES), f32),
-        vmem((na, NY, NZ, R, LANES), bf16),
-        vmem((na, NY, NZ, R, LANES), bf16),
+        vmem((na, R, LANES), bf16),
         vmem((NB, NZ, NY, NX, R, LANES), bf16),
-        vmem((na, mats, R, width), bf16),
+        vmem((NB, mats, R, width), bf16),
         vmem((nd, R, width), bf16),
         vmem((nd * R, width), bf16),
         vmem((nd * R, width), bf16),
@@ -423,8 +385,7 @@
         vmem((nd, 4, 2, NY, R, LANES), f32),
         vmem((nd, NY, R, LANES), f32),
         vmem((nd, NY - 1, R, LANES), f32),
-        vmem((nd, NY, NX, NZ, R, LANES), bf16),
-        vmem((nd, mats, R, width), bf16),
+        vmem((nd, R, LANES), bf16),
         vmem((NY + 1, 8, LANES), i32),
         vmem((NZ, 8, LANES), i32),
         vmem((2, 8, LANES), i32),
@@ -435,8 +396,8 @@
         vmem((rows, LANES), f32),
         vmem((rows, LANES), f32),
         vmem((rows, LANES), bf16),
-        dma((FLIGHT, 12)), dma((na, 12)), dma((FLIGHT, 10)), dma((nd, 10)), dma((2, 4)),
-        dma((3,)), dma((3,)), dma((2,)), dma((2,)), dma((7,)), dma((na + nd, 2)),
+        dma((9,)), dma((12,)), dma((na, 12)), dma((10,)), dma((nd, 10)),
+        dma((3,)), dma((3,)), dma((2,)), dma((2,)), dma((7,)), dma, dma((2, 4)), dma((2,)),
     ]
     anywhere = pl.BlockSpec(memory_space=pl.ANY)
     in_hbm = pl.BlockSpec(memory_space=pltpu.HBM)

time: 86.1 us -> 84.1 us (0.977)
  Pallas kernels: 80.3 us -> 78.1 us
    pallas_call x1, Pallas kernels: 80.3 us -> 78.1 us  [per_device(): pl.pallas_call(functools.partial(kernel, na, nd, rows), out_shape=shapes,...]
where the time goes in v4:
time: 84.1 us; the launch traced here: 83.7 us
  Pallas kernels  78.1 us (93%)
  local copies, waits for them, and re-layouts  2.91 us (3%)
  between operations  1.95 us (2%)
    pallas_call x1, Pallas kernels, per_device(): pl.pallas_call(functools.partial(kernel, na, nd, rows), out_shape=shapes,...  78.1 us
    unnamed x5, local copies, waits for them, and re-layouts  2.91 us

profile of v4, /device:TPU:2, one launch (start us, length us, event | category | flops | bytes accessed | tf_op | source)
XLA Modules:
  0.0 83.7 jit_solution(6137551122580529593)
XLA Ops:
  1.3 0.0 copy-start
  1.3 0.9 %copy-done = f32[2,256,64]{1,2,0:T(8,128)S(1)} copy-done((f32[2,256,64]{1,2,0:T(8,128)S(1)}, f32[2,256,64]{1,2,0:T(8,128)}, u32[]{:S(2)}) %copy-start) | copy-done | bytes 131096
  2.2 0.0 copy-start.1
  2.2 78.1 %shard_map.85 = (bf16[2,256,4096]{2,1,0:T(8,128)(2,1)S(1)}, f32[2,64,256]{2,1,0:T(8,128)S(1)}, f32[2,64,256]{2,1,0:T(8,128)S(1)}) custom-call(bf16[1,2,256,4096]{3,2,1,0:T(8,128)(2,1)} %local.1, bf16[2,256,4096]{2,1,0:T(8,128)(2,1)} %outer.1, f32[2,64,256]{2,1,0:T(8,128)S(1)} %bitcast.10, s32[1]{0:T(128)S(6)} %copy.10.tokens), custom_call_target="tpu_custom_call" | custom-call | tf_op jit(solution)/shard_map/pallas_call | solution.py:407
  80.9 0.0 copy-done.1
  80.9 0.7 fusion.1
  81.7 2.0 %copy.12 = bf16[2,256,4096]{2,1,0:T(8,128)(2,1)} copy(bf16[2,256,4096]{2,1,0:T(8,128)(2,1)S(1)} %get-tuple-element.14) | data formatting | bytes 8388608
Async XLA Ops:
  1.3 0.9 %copy-start = (f32[2,256,64]{1,2,0:T(8,128)S(1)}, f32[2,256,64]{1,2,0:T(8,128)}, u32[]{:S(2)}) copy-start(f32[2,256,64]{1,2,0:T(8,128)} %param.8) | copy-start | bytes 393220
  2.2 78.7 %copy-start.1 = (f32[2,256,64]{1,2,0:T(8,128)S(1)}, f32[2,256,64]{1,2,0:T(8,128)}, u32[]{:S(2)}) copy-start(f32[2,256,64]{1,2,0:T(8,128)} %param.9) | copy-start | bytes 393220

commit v5 on v4

--- a/solution.py
+++ b/solution.py
@@ -12,22 +12,23 @@
 LANES = 128
 R = 16
 AHEAD = 3
-NB = 5
-ND = 7
-A_AT = (0, 1, 2, 3, 4, 5, 6, 8)
-B_AT = (0, 1, 2, 3, 4, 5, 6, 8, 10, 12, 13, 14)
-D_AT = (0, 1, 2, 3, 4, 6, 7, 9, 10)
+NB = 4
+ND = 6
+A_AT = (0, 1, 2, 4, 5, 7)
+B_AT = (0, 1, 3, 4, 5, 6, 8, 10, 12, 13, 15, 17)
+D_AT = (0, 1, 3, 4, 5, 7, 9, 11, 13)
 ORDER = (
-    ("B", 9), ("A", 0), ("A", 1), ("D", 0), ("A", 2), ("A", 3), ("A", 7), ("D", 7), ("A", 4), ("A", 5), ("D", 5), ("B", 8), ("B", 10), ("A", 6), ("D", 1), ("B", 11), ("B", 5), ("B", 7), ("B", 6), ("D", 2), ("D", 8), ("D", 6), ("D", 3), ("D", 4),
+    ("D", 2), ("B", 2), ("A", 0), ("B", 11), ("B", 10), ("B", 8), ("D", 7), ("A", 3), ("D", 6), ("D", 8), ("D", 3), ("B", 3), ("D", 0), ("D", 5), ("B", 9), ("B", 4), ("A", 5), ("D", 4), ("B", 0), ("A", 1), ("B", 5), ("B", 6), ("B", 7), ("A", 4), ("D", 1), ("A", 2), ("B", 1),
 )
 RAW, RING, MID, FIRST, SECOND, LAST = 0, 1, 5, 6, 7, 8
+XSUM, TREE = 1, 2
 
 
 def kernel(
     na, nd, rows,
     local, outer, mom_t, tokens,
     out, grad_t, upd_t,
-    a_raw, a_own, a_out, a_p, a_r, a_q, a_qx, a_v, b_w, b_stage,
+    a_raw, a_own, a_out, a_p, a_x, a_t, a_u, a_v, b_p, a_r, a_q, a_qx, b_w, b_stage,
     d_raw, d_own, d_out, d_p, d_r, d_q, d_qy, d_v,
     cnt, cnt_z, cnt_x, total, gbuf, ubuf, mfull, gfull, ufull, ofull,
     a_ss, b_ss, a_rs, d_ss, d_rs, c_ss, c_rs, m_ss, m_rs, l_sem, o_sem, v_sem, end_s,
@@ -138,8 +139,19 @@
         ufull[rws, :] = upd
         return upd.astype(bf16)
 
+    def a_sums(c):
+        drain(a_raw.at[c], a_rs.at[c, RAW])
+        for zz in range(NZ):
+            for m in range(2):
+                o = a_out[m, a_rows(c), lanes(zz)].astype(f32)
+                acc = cnt_f(0) * (o - a_own[m, a_rows(c), lanes(zz)].astype(f32))
+                for k in range(1, NY):
+                    acc += cnt_f(k) * (o - a_raw[c, k - 1, m, :, lanes(zz)].astype(f32))
+                a_p[c, m, zz] = acc
+
     def a_stage_fn(stage, c):
-        ring = functools.partial(ring_stage, c=c, sign=1 - 2 * (c % 2), p=a_p, r=a_r, ss=a_ss, rs=a_rs)
+        e = c - NB
+        sign = 1 - 2 * (c % 2)
 
         def sems(k):
             return a_ss.at[k], a_rs.at[c, k]
@@ -148,31 +160,32 @@
             drain(ref, a_rs.at[c, k])
 
         if stage == 0:
-            landed(a_raw.at[c], RAW)
-            for zz in range(NZ):
-                for m in range(2):
-                    o = a_out[m, a_rows(c), lanes(zz)].astype(f32)
-                    acc = cnt_f(0) * (o - a_own[m, a_rows(c), lanes(zz)].astype(f32))
-                    for k in range(1, NY):
-                        acc += cnt_f(k) * (o - a_raw[c, k - 1, m, :, lanes(zz)].astype(f32))
-                    a_p[c, zz, m] = acc
-            ring(0)
-        elif stage <= 3:
-            ring(stage)
+            a_sums(c)
+            send(a_p.at[c, other], a_x.at[e], *sems(XSUM), partner)
+        elif stage == 1:
+            landed(a_x.at[e], XSUM)
+            a_x[e] += a_p[c, x]
+            send(a_x.at[e, zi(4 * sign)], a_t.at[e, 0], *sems(TREE), at(y, z + 2 * sign, x))
+            send(a_x.at[e, zi(3 * sign)], a_t.at[e, 1], *sems(TREE), at(y, z + sign, x))
+            send(a_x.at[e, zi(-3 * sign)], a_t.at[e, 2], *sems(TREE), at(y, z - sign, x))
+        elif stage == 2:
+            landed(a_t.at[e], TREE)
+            a_t[e, 0] += a_t[e, 1] + a_x[e, zi(2 * sign)]
+            a_t[e, 2] += a_x[e, zi(-2 * sign)]
+            send(a_t.at[e, 0], a_u.at[e, 0], *sems(TREE + 1), at(y, z + 2 * sign, x))
+            send(a_t.at[e, 2], a_u.at[e, 1], *sems(TREE + 1), at(y, z - 2 * sign, x))
+            send(a_x.at[e, zi(sign)], a_u.at[e, 2], *sems(TREE + 1), at(y, z + sign, x))
+            send(a_x.at[e, zi(-sign)], a_u.at[e, 3], *sems(TREE + 1), at(y, z - sign, x))
+        elif stage == 3:
+            landed(a_u.at[e], TREE + 1)
+            a_v[e] = update(a_rows(c), a_x[e, z] + ((a_u[e, 0] + a_u[e, 1]) + (a_u[e, 2] + a_u[e, 3])))
+            place = out.at[x, a_rows(c), cols]
+            pltpu.make_async_copy(a_v.at[e], place, v_sem.at[0, c % 4]).start()
+            for k in (4, 3, 5, 2, 6, 1, 7):
+                send(a_v.at[e], place, *sems(FIRST), z_peers[k - 1])
         elif stage == 4:
-            ring(4)
-            a_q[c] = a_p[c, z] + a_r[c, 3, 0] + a_r[c, 2, 1]
-            send(a_q.at[c, other], a_qx.at[c], *sems(MID), partner)
-        elif stage == 5:
-            landed(a_qx.at[c], MID)
-            a_v[c] = update(a_rows(c), a_q[c, x] + a_qx[c])
-            place = out.at[x, a_rows(c), cols]
-            pltpu.make_async_copy(a_v.at[c], place, v_sem.at[0, c % 4]).start()
-            for k in (4, 3, 5, 2, 6, 1, 7):
-                send(a_v.at[c], place, *sems(FIRST), z_peers[k - 1])
-        elif stage == 6:
             landed(out.at[x, a_rows(c), pl.ds(0, (NZ - 1) * LANES)], FIRST)
-            drain(a_v.at[c], v_sem.at[0, c % 4])
+            drain(a_v.at[e], v_sem.at[0, c % 4])
             place = out.at[x, a_rows(c), ycols]
             for k in (2, 1, 3):
                 send(place, place, *sems(SECOND), y_peers[k - 1])
@@ -197,7 +210,20 @@
             if k < 3:
                 send(short, short, *sems(LAST + k), down)
 
-        if stage == 5:
+        ring = functools.partial(ring_stage, c=c, sign=sign, p=b_p, r=a_r, ss=b_ss, rs=a_rs)
+        if stage == 0:
+            a_sums(c)
+            for zz in range(NZ):
+                for m in range(2):
+                    b_p[c, zz, m] = a_p[c, m, zz]
+            ring(0)
+        elif stage <= 3:
+            ring(stage)
+        elif stage == 4:
+            ring(4)
+            a_q[c] = b_p[c, z] + a_r[c, 3, 0] + a_r[c, 2, 1]
+            send(a_q.at[c, other], a_qx.at[c], *sems(MID), partner)
+        elif stage == 5:
             landed(a_qx.at[c], MID)
             mine = b_w.at[c, z, y, x]
             mine[...] = update(a_rows(c), a_q[c, x] + a_qx[c])
@@ -316,11 +342,11 @@
             elif kind == "B":
                 c, low, high, fn = t - B_AT[stage], 0, NB, b_stage_fn
             else:
-                c, low, high, fn = t - A_AT[stage], NB if stage > 4 else 0, na, a_stage_fn
+                c, low, high, fn = t - A_AT[stage], NB, na, a_stage_fn
             pl.when((c >= low) & (c < high))(functools.partial(fn, stage, c))
         send_raw(t + AHEAD)
 
-        @pl.when(t == max(na + A_AT[5], NB + B_AT[5], nd + D_AT[5]))
+        @pl.when(t == max(na + A_AT[3], NB + B_AT[5], nd + D_AT[5]))
         def _():
             gbuf[...] = gfull[...].T
             ubuf[...] = ufull[...].T
@@ -344,7 +370,8 @@
 
     for ref, sem in [
         (part(1, na - NB, NY * NZ), end_s.at[0]), (part(1, nd, 2 * NZ), end_s.at[1]), (part(2, NB, NY * NZ), o_sem),
-        (a_raw, a_ss.at[RAW]), (a_r.at[:, 3, 0], a_ss.at[RING + 3]), (a_qx, a_ss.at[MID]),
+        (a_raw, a_ss.at[RAW]), (a_x, a_ss.at[XSUM]), (a_t, a_ss.at[TREE]), (a_u, a_ss.at[TREE + 1]),
+        (a_r.at[:, 3, 0], b_ss.at[RING + 3]), (a_qx, b_ss.at[MID]),
         (part(1, na - NB, NZ - 1), a_ss.at[FIRST]), (part(1, na - NB, (NY - 1) * NZ), a_ss.at[SECOND]),
         (part(1, na - NB, NY * NZ), a_ss.at[LAST]),
         (b_w.at[:, 0, 0, 0], b_ss.at[FIRST]), (b_w.at[:, 0, pl.ds(0, NY - 1)], b_ss.at[SECOND]),
@@ -355,7 +382,7 @@
     ]:
         drain(ref, sem)
     for k in range(3):
-        drain(a_r.at[:, k], a_ss.at[RING + k])
+        drain(a_r.at[:, k], b_ss.at[RING + k])
         drain(b_w.at[:, pl.ds(0, 2)], b_ss.at[LAST + k])
         drain(d_r.at[:, k], d_ss.at[RING + k])
 
@@ -371,11 +398,15 @@
         vmem((na, NY - 1, mats, R, wide), bf16),
         vmem((mats, na * R, wide), bf16),
         vmem((mats, na * R, wide), bf16),
-        vmem((na, NZ, mats, R, LANES), f32),
-        vmem((na, 4, 2, mats, R, LANES), f32),
-        vmem((na, mats, R, LANES), f32),
-        vmem((na, R, LANES), f32),
-        vmem((na, R, LANES), bf16),
+        vmem((na, mats, NZ, R, LANES), f32),
+        vmem((na - NB, NZ, R, LANES), f32),
+        vmem((na - NB, 3, R, LANES), f32),
+        vmem((na - NB, 4, R, LANES), f32),
+        vmem((na - NB, R, LANES), bf16),
+        vmem((NB, NZ, mats, R, LANES), f32),
+        vmem((NB, 4, 2, mats, R, LANES), f32),
+        vmem((NB, mats, R, LANES), f32),
+        vmem((NB, R, LANES), f32),
         vmem((NB, NZ, NY, NX, R, LANES), bf16),
         vmem((NB, mats, R, width), bf16),
         vmem((nd, R, width), bf16),

time: 84.1 us -> 79.4 us (0.944)
  Pallas kernels: 78.1 us -> 73.7 us
    pallas_call x1, Pallas kernels: 78.1 us -> 73.7 us  [per_device(): pl.pallas_call(functools.partial(kernel, na, nd, rows), out_shape=shapes,...]
where the time goes in v5:
time: 79.4 us; the launch traced here: 79.3 us
  Pallas kernels  73.7 us (93%)
  local copies, waits for them, and re-layouts  2.91 us (4%)
  between operations  1.95 us (2%)
    pallas_call x1, Pallas kernels, per_device(): pl.pallas_call(functools.partial(kernel, na, nd, rows), out_shape=shapes,...  73.7 us
    unnamed x5, local copies, waits for them, and re-layouts  2.91 us

profile of v5, /device:TPU:2, one launch (start us, length us, event | category | flops | bytes accessed | tf_op | source)
XLA Modules:
  0.0 79.3 jit_solution(2526717786305334206)
XLA Ops:
  1.3 0.0 copy-start
  1.3 0.9 %copy-done = f32[2,256,64]{1,2,0:T(8,128)S(1)} copy-done((f32[2,256,64]{1,2,0:T(8,128)S(1)}, f32[2,256,64]{1,2,0:T(8,128)}, u32[]{:S(2)}) %copy-start) | copy-done | bytes 131096
  2.2 0.0 copy-start.1
  2.2 73.7 %shard_map.85 = (bf16[2,256,4096]{2,1,0:T(8,128)(2,1)S(1)}, f32[2,64,256]{2,1,0:T(8,128)S(1)}, f32[2,64,256]{2,1,0:T(8,128)S(1)}) custom-call(bf16[1,2,256,4096]{3,2,1,0:T(8,128)(2,1)} %local.1, bf16[2,256,4096]{2,1,0:T(8,128)(2,1)} %outer.1, f32[2,64,256]{2,1,0:T(8,128)S(1)} %bitcast.10, s32[1]{0:T(128)S(6)} %copy.10.tokens), custom_call_target="tpu_custom_call" | custom-call | tf_op jit(solution)/shard_map/pallas_call | solution.py:438
  76.6 0.0 copy-done.1
  76.6 0.7 fusion.1
  77.3 2.0 %copy.12 = bf16[2,256,4096]{2,1,0:T(8,128)(2,1)} copy(bf16[2,256,4096]{2,1,0:T(8,128)(2,1)S(1)} %get-tuple-element.14) | data formatting | bytes 8388608
Async XLA Ops:
  1.3 0.9 %copy-start = (f32[2,256,64]{1,2,0:T(8,128)S(1)}, f32[2,256,64]{1,2,0:T(8,128)}, u32[]{:S(2)}) copy-start(f32[2,256,64]{1,2,0:T(8,128)} %param.8) | copy-start | bytes 393220
  2.2 74.4 %copy-start.1 = (f32[2,256,64]{1,2,0:T(8,128)S(1)}, f32[2,256,64]{1,2,0:T(8,128)}, u32[]{:S(2)}) copy-start(f32[2,256,64]{1,2,0:T(8,128)} %param.9) | copy-start | bytes 393220

commit v6 on v5

--- a/solution.py
+++ b/solution.py
@@ -31,7 +31,7 @@
     a_raw, a_own, a_out, a_p, a_x, a_t, a_u, a_v, b_p, a_r, a_q, a_qx, b_w, b_stage,
     d_raw, d_own, d_out, d_p, d_r, d_q, d_qy, d_v,
     cnt, cnt_z, cnt_x, total, gbuf, ubuf, mfull, gfull, ufull, ofull,
-    a_ss, b_ss, a_rs, d_ss, d_rs, c_ss, c_rs, m_ss, m_rs, l_sem, o_sem, v_sem, end_s,
+    a_ss, b_ss, a_rs, b_rs, d_ss, d_rs, c_ss, c_rs, m_ss, m_rs, l_sem, o_sem, v_sem, end_s,
 ):
     f32, bf16 = jnp.float32, jnp.bfloat16
     rep, fsdp = lax.axis_index("rep"), lax.axis_index("fsdp")
@@ -139,7 +139,7 @@
         ufull[rws, :] = upd
         return upd.astype(bf16)
 
-    def a_sums(c):
+    def a_sums(c, keep):
         drain(a_raw.at[c], a_rs.at[c, RAW])
         for zz in range(NZ):
             for m in range(2):
@@ -147,7 +147,7 @@
                 acc = cnt_f(0) * (o - a_own[m, a_rows(c), lanes(zz)].astype(f32))
                 for k in range(1, NY):
                     acc += cnt_f(k) * (o - a_raw[c, k - 1, m, :, lanes(zz)].astype(f32))
-                a_p[c, m, zz] = acc
+                keep(m, zz, acc)
 
     def a_stage_fn(stage, c):
         e = c - NB
@@ -160,11 +160,14 @@
             drain(ref, a_rs.at[c, k])
 
         if stage == 0:
-            a_sums(c)
-            send(a_p.at[c, other], a_x.at[e], *sems(XSUM), partner)
+            def keep(m, zz, acc):
+                a_p[e, m, zz] = acc
+
+            a_sums(c, keep)
+            send(a_p.at[e, other], a_x.at[e], *sems(XSUM), partner)
         elif stage == 1:
             landed(a_x.at[e], XSUM)
-            a_x[e] += a_p[c, x]
+            a_x[e] += a_p[e, x]
             send(a_x.at[e, zi(4 * sign)], a_t.at[e, 0], *sems(TREE), at(y, z + 2 * sign, x))
             send(a_x.at[e, zi(3 * sign)], a_t.at[e, 1], *sems(TREE), at(y, z + sign, x))
             send(a_x.at[e, zi(-3 * sign)], a_t.at[e, 2], *sems(TREE), at(y, z - sign, x))
@@ -206,16 +209,17 @@
 
         def step(k):
             long, short = b_w.at[c, zi(-k * sign)], b_w.at[c, zi(k * sign)]
-            send(long, long, *sems(LAST + k), up)
+            send(long, long, b_ss.at[LAST + k], b_rs.at[c, k], up)
             if k < 3:
-                send(short, short, *sems(LAST + k), down)
+                send(short, short, b_ss.at[LAST + k], b_rs.at[c, k], down)
 
         ring = functools.partial(ring_stage, c=c, sign=sign, p=b_p, r=a_r, ss=b_ss, rs=a_rs)
         if stage == 0:
-            a_sums(c)
-            for zz in range(NZ):
-                for m in range(2):
-                    b_p[c, zz, m] = a_p[c, m, zz]
+
+            def keep(m, zz, acc):
+                b_p[c, zz, m] = acc
+
+            a_sums(c, keep)
             ring(0)
         elif stage <= 3:
             ring(stage)
@@ -239,7 +243,7 @@
         else:
             k = stage - 8
             came = b_w.at[c, pl.ds(0, 2 if k < 3 else 1)]
-            landed(came, LAST + k)
+            drain(came, b_rs.at[c, k])
             if k < 3:
                 step(k + 1)
             else:
@@ -398,7 +402,7 @@
         vmem((na, NY - 1, mats, R, wide), bf16),
         vmem((mats, na * R, wide), bf16),
         vmem((mats, na * R, wide), bf16),
-        vmem((na, mats, NZ, R, LANES), f32),
+        vmem((na - NB, mats, NZ, R, LANES), f32),
         vmem((na - NB, NZ, R, LANES), f32),
         vmem((na - NB, 3, R, LANES), f32),
         vmem((na - NB, 4, R, LANES), f32),
@@ -427,7 +431,7 @@
         vmem((rows, LANES), f32),
         vmem((rows, LANES), f32),
         vmem((rows, LANES), bf16),
-        dma((9,)), dma((12,)), dma((na, 12)), dma((10,)), dma((nd, 10)),
+        dma((9,)), dma((12,)), dma((na, 8)), dma((NB, 4)), dma((10,)), dma((nd, 9)),
         dma((3,)), dma((3,)), dma((2,)), dma((2,)), dma((7,)), dma, dma((2, 4)), dma((2,)),
     ]
     anywhere = pl.BlockSpec(memory_space=pl.ANY)

time: 79.4 us -> 79.2 us (level)
  no operation moved by 1% of the time
where the time goes in v6:
time: 79.2 us; the launch traced here: 79.1 us
  Pallas kernels  73.5 us (93%)
  local copies, waits for them, and re-layouts  2.91 us (4%)
  between operations  1.95 us (2%)
    pallas_call x1, Pallas kernels, per_device(): pl.pallas_call(functools.partial(kernel, na, nd, rows), out_shape=shapes,...  73.5 us
    unnamed x5, local copies, waits for them, and re-layouts  2.91 us

profile of v6, /device:TPU:2, one launch (start us, length us, event | category | flops | bytes accessed | tf_op | source)
XLA Modules:
  0.0 79.1 jit_solution(8224018358998291758)
XLA Ops:
  1.3 0.0 copy-start
  1.3 0.9 %copy-done = f32[2,256,64]{1,2,0:T(8,128)S(1)} copy-done((f32[2,256,64]{1,2,0:T(8,128)S(1)}, f32[2,256,64]{1,2,0:T(8,128)}, u32[]{:S(2)}) %copy-start) | copy-done | bytes 131096
  2.2 0.0 copy-start.1
  2.2 73.5 %shard_map.85 = (bf16[2,256,4096]{2,1,0:T(8,128)(2,1)S(1)}, f32[2,64,256]{2,1,0:T(8,128)S(1)}, f32[2,64,256]{2,1,0:T(8,128)S(1)}) custom-call(bf16[1,2,256,4096]{3,2,1,0:T(8,128)(2,1)} %local.1, bf16[2,256,4096]{2,1,0:T(8,128)(2,1)} %outer.1, f32[2,64,256]{2,1,0:T(8,128)S(1)} %bitcast.10, s32[1]{0:T(128)S(6)} %copy.10.tokens), custom_call_target="tpu_custom_call" | custom-call | tf_op jit(solution)/shard_map/pallas_call | solution.py:442
  76.3 0.0 copy-done.1
  76.3 0.7 fusion.1
  77.0 2.0 %copy.12 = bf16[2,256,4096]{2,1,0:T(8,128)(2,1)} copy(bf16[2,256,4096]{2,1,0:T(8,128)(2,1)S(1)} %get-tuple-element.14) | data formatting | bytes 8388608
Async XLA Ops:
  1.3 0.9 %copy-start = (f32[2,256,64]{1,2,0:T(8,128)S(1)}, f32[2,256,64]{1,2,0:T(8,128)}, u32[]{:S(2)}) copy-start(f32[2,256,64]{1,2,0:T(8,128)} %param.8) | copy-start | bytes 393220
  2.2 74.1 %copy-start.1 = (f32[2,256,64]{1,2,0:T(8,128)S(1)}, f32[2,256,64]{1,2,0:T(8,128)}, u32[]{:S(2)}) copy-start(f32[2,256,64]{1,2,0:T(8,128)} %param.9) | copy-start | bytes 393220

commit v7 on v6

--- a/solution.py
+++ b/solution.py
@@ -373,7 +373,7 @@
         return out.at[pl.ds(0, mats), pl.ds(0, chunks * R), pl.ds(0, blocks * LANES)]
 
     for ref, sem in [
-        (part(1, na - NB, NY * NZ), end_s.at[0]), (part(1, nd, 2 * NZ), end_s.at[1]), (part(2, NB, NY * NZ), o_sem),
+        (part(2, NB, NY * NZ), o_sem),
         (a_raw, a_ss.at[RAW]), (a_x, a_ss.at[XSUM]), (a_t, a_ss.at[TREE]), (a_u, a_ss.at[TREE + 1]),
         (a_r.at[:, 3, 0], b_ss.at[RING + 3]), (a_qx, b_ss.at[MID]),
         (part(1, na - NB, NZ - 1), a_ss.at[FIRST]), (part(1, na - NB, (NY - 1) * NZ), a_ss.at[SECOND]),
@@ -389,6 +389,8 @@
         drain(a_r.at[:, k], b_ss.at[RING + k])
         drain(b_w.at[:, pl.ds(0, 2)], b_ss.at[LAST + k])
         drain(d_r.at[:, k], d_ss.at[RING + k])
+    drain(part(1, na - NB, NY * NZ), end_s.at[0])
+    drain(part(1, nd, 2 * NZ), end_s.at[1])
 
 
 def per_device(local, outer, momentum, swa, tokens, step_no):

time: 79.2 us -> 79.1 us (level)
  no operation moved by 1% of the time
where the time goes in v7:
time: 79.1 us; the launch traced here: 79 us
  Pallas kernels  73.4 us (93%)
  local copies, waits for them, and re-layouts  2.91 us (4%)
  between operations  1.95 us (2%)
    pallas_call x1, Pallas kernels, per_device(): pl.pallas_call(functools.partial(kernel, na, nd, rows), out_shape=shapes,...  73.4 us
    unnamed x5, local copies, waits for them, and re-layouts  2.91 us

profile of v7, /device:TPU:2, one launch (start us, length us, event | category | flops | bytes accessed | tf_op | source)
XLA Modules:
  0.0 79.0 jit_solution(5756593468509924026)
XLA Ops:
  1.3 0.0 copy-start
  1.3 0.9 %copy-done = f32[2,256,64]{1,2,0:T(8,128)S(1)} copy-done((f32[2,256,64]{1,2,0:T(8,128)S(1)}, f32[2,256,64]{1,2,0:T(8,128)}, u32[]{:S(2)}) %copy-start) | copy-done | bytes 131096
  2.2 0.0 copy-start.1
  2.2 73.4 %shard_map.85 = (bf16[2,256,4096]{2,1,0:T(8,128)(2,1)S(1)}, f32[2,64,256]{2,1,0:T(8,128)S(1)}, f32[2,64,256]{2,1,0:T(8,128)S(1)}) custom-call(bf16[1,2,256,4096]{3,2,1,0:T(8,128)(2,1)} %local.1, bf16[2,256,4096]{2,1,0:T(8,128)(2,1)} %outer.1, f32[2,64,256]{2,1,0:T(8,128)S(1)} %bitcast.10, s32[1]{0:T(128)S(6)} %copy.10.tokens), custom_call_target="tpu_custom_call" | custom-call | tf_op jit(solution)/shard_map/pallas_call | solution.py:444
  76.3 0.0 copy-done.1
  76.3 0.7 fusion.1
  77.0 2.0 %copy.12 = bf16[2,256,4096]{2,1,0:T(8,128)(2,1)} copy(bf16[2,256,4096]{2,1,0:T(8,128)(2,1)S(1)} %get-tuple-element.14) | data formatting | bytes 8388608
Async XLA Ops:
  1.3 0.9 %copy-start = (f32[2,256,64]{1,2,0:T(8,128)S(1)}, f32[2,256,64]{1,2,0:T(8,128)}, u32[]{:S(2)}) copy-start(f32[2,256,64]{1,2,0:T(8,128)} %param.8) | copy-start | bytes 393220
  2.2 74.1 %copy-start.1 = (f32[2,256,64]{1,2,0:T(8,128)S(1)}, f32[2,256,64]{1,2,0:T(8,128)}, u32[]{:S(2)}) copy-start(f32[2,256,64]{1,2,0:T(8,128)} %param.9) | copy-start | bytes 393220
